TPU v7x, 256 devices: a whole 4x4x8 slice. The times are simulated.
256 devices in a mesh: strip: 32 (over z, y_lo, core), basis: 8 (over x, y_hi).
Axes of the slice: x: 4, y: 4 (y_hi: 2, y_lo: 2; y = y_hi * 2 + y_lo), z: 8, core: 2. Of those that a mesh axis runs over, the one named last changes fastest.
Arguments:
- sky_image: float32 [4096, 1024], P('strip', 'basis'), may hold values from -6 to 6
- dual_coeffs: float32 [8, 4096, 1024], P('basis', 'strip'), may hold values from -2 to 2
- thresholds: float32 [8, 4096, 1024], P('basis', 'strip'), may hold values from 0.05 to 1
Outputs:
- dual_next: float32 [8, 4096, 1024], P('basis', 'strip')
- adjoint_image: float32 [4096, 1024], P('strip', 'basis')
All inputs are finite; a program needn't handle non-finite values.
Results may differ from a plain program's by a relative error of at most 0.00002.
Values sent between devices are 32-bit elements; how exact they have to be, the bound alone decides.
No kernel may reach another device: no remote copies, remote signals or barrier semaphores. Data moves between devices by JAX's collectives and lax.ppermute only.
A program may use at most 64 MiB of HBM per device.

v0:
```python
import math

import jax
import jax.numpy as jnp
import numpy as np
from jax import lax
from jax.experimental import pallas as pl
from jax.experimental.pallas import tpu as pltpu
from jax.sharding import PartitionSpec as P

BASES = 8
ROWS = 128
COLS = 1024
TILE = 256
TAIL = 104
EXT = ROWS + TAIL
BANDS = 224


daubechies = [
    [0.7071067811865476, 0.7071067811865476],
    [0.48296291314469025, 0.836516303737469, 0.22414386804185735, -0.12940952255092145],
    [
        0.3326705529509569,
        0.8068915093133388,
        0.4598775021193313,
        -0.13501102001039084,
        -0.08544127388224149,
        0.035226291882100656,
    ],
    [
        0.23037781330885523,
        0.7148465705525415,
        0.6308807679295904,
        -0.02798376941698385,
        -0.18703481171888114,
        0.030841381835986965,
        0.032883011666982945,
        -0.010597401784997278,
    ],
    [
        0.160102397974125,
        0.6038292697974729,
        0.7243085284385744,
        0.13842814590110342,
        -0.24229488706619015,
        -0.03224486958502952,
        0.07757149384006515,
        -0.006241490213011705,
        -0.012580751999015526,
        0.003335725285001549,
    ],
    [
        0.11154074335008017,
        0.4946238903983854,
        0.7511339080215775,
        0.3152503517092432,
        -0.22626469396516913,
        -0.12976686756709563,
        0.09750160558707936,
        0.02752286553001629,
        -0.031582039318031156,
        0.0005538422009938016,
        0.004777257511010651,
        -0.00107730108499558,
    ],
    [
        0.07785205408506236,
        0.39653931948230575,
        0.7291320908465551,
        0.4697822874053586,
        -0.14390600392910627,
        -0.22403618499416572,
        0.07130921926705004,
        0.08061260915106681,
        -0.03802993693503463,
        -0.01657454163101562,
        0.012550998556013784,
        0.00042957797300470274,
        -0.0018016407039998328,
        0.0003537138000010399,
    ],
    [
        0.05441584224308161,
        0.3128715909144659,
        0.6756307362980128,
        0.5853546836548691,
        -0.015829105256023893,
        -0.2840155429624281,
        0.00047248457399797254,
        0.128747426620186,
        -0.01736930100202211,
        -0.04408825393106472,
        0.013981027917015516,
        0.008746094047015655,
        -0.00487035299301066,
        -0.0003917403729959771,
        0.0006754494059985568,
        -0.00011747678400228192,
    ],
]


def composed_filters():
    filters = []
    for taps in daubechies:
        length = len(taps)
        low = np.zeros(16)
        high = np.zeros(16)
        low[:length] = np.float32(taps)
        high[:length] = [(-1) ** k * np.float32(taps[length - 1 - k]) for k in range(length)]
        levels = [(low, high)]
        for level in (1, 2):
            coarse = levels[-1][0]
            step = 2**level
            size = len(coarse) + 15 * step
            pair = []
            for band in (low, high):
                longer = np.zeros(size)
                for k in range(16):
                    longer[k * step : k * step + len(coarse)] += band[k] * coarse
                pair.append(longer)
            levels.append(tuple(pair))
        filters.append(levels)
    return filters


def row_and_column_matrices():
    scale = 1.0 / math.sqrt(BASES)
    odd = list(range(1, ROWS, 2))
    two = list(range(2, ROWS, 4))
    four = list(range(0, ROWS, 4))
    order = [(1, r) for r in odd + two + four] + [(2, r) for r in two + four] + [(3, r) for r in four]
    rows = np.zeros((BASES, BANDS, EXT))
    columns = np.zeros((BASES, 3, TILE + 128, TILE))
    for basis, levels in enumerate(composed_filters()):
        for at, (level, row) in enumerate(order):
            half = 2 ** (level - 1)
            taps = levels[level - 1][(row // half) % 2]
            start = row - row % (2 * half)
            rows[basis, at, start : start + len(taps)] += taps * scale
        for level in (1, 2, 3):
            half = 2 ** (level - 1)
            for column in range(0, TILE, half):
                taps = levels[level - 1][(column // half) % 2]
                start = column - column % (2 * half)
                columns[basis, level - 1, start : start + len(taps), column] += taps
    return rows.astype(np.float32), columns.astype(np.float32)


def matmul(a, b):
    return lax.dot_general(
        a, b, (((1,), (0,)), ((), ())), precision=lax.Precision.HIGHEST, preferred_element_type=jnp.float32
    )


def matmul_t(a, b):
    return lax.dot_general(
        a, b, (((1,), (1,)), ((), ())), precision=lax.Precision.HIGHEST, preferred_element_type=jnp.float32
    )


def left_matmul_t(a, b):
    return lax.dot_general(
        a, b, (((0,), (0,)), ((), ())), precision=lax.Precision.HIGHEST, preferred_element_type=jnp.float32
    )


LEVEL_ROWS = ((0, 128), (128, 64), (192, 32))


def wavelet_kernel(basis_ref, image_ref, dual_ref, limit_ref, rows_ref, columns_ref, next_ref, adjoint_ref, bands, masked, woven):
    tiles = COLS // TILE
    row_op = rows_ref[0]
    for t in range(tiles):
        field = jnp.concatenate([image_ref[2 * t], image_ref[2 * t + 1]], axis=1)
        bands[:, t * TILE : (t + 1) * TILE] = matmul(row_op, field)
    column = lax.broadcasted_iota(jnp.int32, (32, TILE), 1)
    even = column % 2 == 0
    fourth = column % 4 == 0
    for t in range(tiles):
        at = slice(t * TILE, (t + 1) * TILE)
        ahead = (t + 1) % tiles * TILE
        out = []
        for level, (first, count) in enumerate(LEVEL_ROWS):
            main = matmul(bands[first : first + count, at], columns_ref[0, level, :TILE, :])
            rim = matmul(bands[first : first + count, ahead : ahead + 128], columns_ref[0, level, TILE:, 128:])
            out.append(jnp.concatenate([main[:, :128], main[:, 128:] + rim], axis=1))
        one, two, three = out
        coarse = (
            (1, 2, one[:64]),
            (2, 4, jnp.where(even, two[:32], one[64:96])),
            (0, 4, jnp.where(fourth, three, jnp.where(even, two[32:], one[96:]))),
        )
        halves = ((0, slice(0, 128)), (1, slice(128, TILE)))
        for first, stride, value in coarse:
            for h, lanes in halves:
                woven[2 * t + h, pl.ds(first, ROWS // stride, stride), :] = value[:, lanes]
        for h in range(2):
            here = slice((2 * t + h) * 128, (2 * t + h + 1) * 128)
            limit = limit_ref[0, :, here]
            fresh = jnp.minimum(jnp.maximum(dual_ref[0, :, here] + woven[2 * t + h], -limit), limit)
            next_ref[0, :, here] = fresh
            woven[2 * t + h] = fresh
        a, b, c = (
            jnp.concatenate([woven[2 * t + h, pl.ds(first, ROWS // stride, stride), :] for h in range(2)], axis=1)
            for first, stride, _ in coarse
        )
        masked[0:64, at] = a
        masked[64:96, at] = jnp.where(even, 0.0, b)
        masked[96:128, at] = jnp.where(even, 0.0, c)
        masked[128:160, at] = b
        masked[160:192, at] = jnp.where(fourth, 0.0, c)
        masked[192:224, at] = c
    for t in range(tiles):
        at = slice(t * TILE, (t + 1) * TILE)
        behind = (t + tiles - 1) % tiles * TILE + 128
        out = []
        for level, (first, count) in enumerate(LEVEL_ROWS):
            main = matmul_t(masked[first : first + count, at], columns_ref[0, level, :TILE, :])
            rim = matmul_t(masked[first : first + count, behind : behind + 128], columns_ref[0, level, TILE:, 128:])
            out.append(jnp.concatenate([main[:, :128] + rim, main[:, 128:]], axis=1))
        part = left_matmul_t(row_op, jnp.concatenate(out, axis=0))
        adjoint_ref[2 * t] = part[:, :128]
        adjoint_ref[2 * t + 1] = part[:, 128:]


def wavelet_update(basis, field, dual_coeffs, thresholds, row_ops, column_ops):
    whole = lambda shape: pl.BlockSpec(shape, lambda i, b: (0,) * len(shape))
    of_basis = lambda shape: pl.BlockSpec(shape, lambda i, b: (b[0],) + (0,) * (len(shape) - 1))
    grid_spec = pltpu.PrefetchScalarGridSpec(
        num_scalar_prefetch=1,
        grid=(1,),
        in_specs=[
            whole((8, EXT, 128)),
            whole((1, ROWS, COLS)),
            whole((1, ROWS, COLS)),
            of_basis((1, BANDS, EXT)),
            of_basis((1, 3, TILE + 128, TILE)),
        ],
        out_specs=[whole((1, ROWS, COLS)), whole((8, EXT, 128))],
        scratch_shapes=[
            pltpu.VMEM((BANDS, COLS), jnp.float32),
            pltpu.VMEM((BANDS, COLS), jnp.float32),
            pltpu.VMEM((8, ROWS, 128), jnp.float32),
        ],
    )
    return pl.pallas_call(
        wavelet_kernel,
        grid_spec=grid_spec,
        out_shape=(
            jax.ShapeDtypeStruct((1, ROWS, COLS), jnp.float32),
            jax.ShapeDtypeStruct((8, EXT, 128), jnp.float32),
        ),
        compiler_params=pltpu.CompilerParams(vmem_limit_bytes=48 * 1024 * 1024),
        name="wavelet_update",
    )(basis, field, dual_coeffs, thresholds, row_ops, column_ops)


def shifted(value, steps):
    count = lax.axis_size("strip")
    pairs = [(source, (source + steps) % count) for source in range(count)]
    return lax.ppermute(value, "strip", pairs)


def on_device(sky_image, dual_coeffs, thresholds):
    row_ops, column_ops = row_and_column_matrices()
    basis = lax.axis_index("basis").astype(jnp.int32).reshape(1)
    with jax.named_scope("rows_of_next_strip"):
        tail = shifted(sky_image[:TAIL], -1)
    with jax.named_scope("gather_columns"):
        block = jnp.concatenate([sky_image, tail], axis=0)
        field = lax.all_to_all(jnp.broadcast_to(block, (BASES, EXT, 128)), "basis", 0, 0)
    dual_next, adjoint = wavelet_update(
        basis, field, dual_coeffs, thresholds, jnp.asarray(row_ops), jnp.asarray(column_ops)
    )
    with jax.named_scope("sum_over_bases"):
        summed = jnp.sum(lax.all_to_all(adjoint, "basis", 0, 0), axis=0)
    with jax.named_scope("rows_to_next_strip"):
        carried = shifted(summed[ROWS:], 1)
        adjoint_image = summed[:ROWS] + jnp.pad(carried, ((0, ROWS - TAIL), (0, 0)))
    return (dual_next, adjoint_image)


def solution(mesh):
    placed = (P("strip", "basis"), P("basis", "strip", None), P("basis", "strip", None))
    return jax.shard_map(
        on_device,
        mesh=mesh,
        in_specs=placed,
        out_specs=(P("basis", "strip", None), P("strip", "basis")),
        check_vma=False,
    )
```

profile of v0, /device:TPU:128, one launch (start us, length us, event | category | flops | bytes accessed | tf_op | source)
XLA Modules:
  0.0 70.1 jit_solution(17979463197191882454)
XLA Ops:
  0.6 0.8 %slice.9 = f32[104,128]{1,0:T(8,128)S(1)} slice(f32[128,128]{1,0:T(8,128)} %param.5), slice={[0:104], [0:128]} | slice | bytes 106496 | tf_op jit(solution)/shard_map/rows_of_next_strip/slice | solution.py:270
  1.4 0.6 collective-permute-start
  2.0 1.8 %collective-permute-done = f32[104,128]{1,0:T(8,128)S(1)} collective-permute-done((f32[104,128]{1,0:T(8,128)S(1)}, f32[104,128]{1,0:T(8,128)S(1)}, u32[]{:S(2)}, u32[]{:S(2)}) %collective-permute-start) | collective-permute-done | bytes 53280 | tf_op jit(solution)/shard_map/rows_of_next_strip/ppermute | solution.py:263
  3.8 0.8 %pad_maximum_fusion = f32[232,128]{1,0:T(8,128)S(1)} fusion(f32[104,128]{1,0:T(8,128)S(1)} %collective-permute-done, f32[128,128]{1,0:T(8,128)} %param.5), kind=kLoop, calls=%fused_computation | loop fusion | flops 29696 | bytes 237568 | tf_op jit(solution)/shard_map/gather_columns/concatenate | solution.py:272
  4.6 1.0 %broadcast_in_dim.3 = f32[8,232,128]{2,1,0:T(8,128)} broadcast(f32[232,128]{1,0:T(8,128)S(1)} %pad_maximum_fusion), dimensions={1,2} | broadcast | bytes 1069056 | tf_op jit(solution)/shard_map/gather_columns/broadcast_in_dim | solution.py:273
  5.7 6.6 %all-to-all-start = ((f32[8,232,128]{2,1,0:T(8,128)}), f32[8,232,128]{2,1,0:T(8,128)S(1)}, u32[]{:S(2)}, u32[]{:S(2)}) async-start(f32[8,232,128]{2,1,0:T(8,128)} %broadcast_in_dim.3), calls=%async_computation | async-start | bytes 1900544 | tf_op jit(solution)/shard_map/gather_columns/all_to_all | solution.py:273
  12.3 17.1 %all-to-all-done.image_ref = f32[8,232,128]{2,1,0:T(8,128)S(1)} async-done(((f32[8,232,128]{2,1,0:T(8,128)}), f32[8,232,128]{2,1,0:T(8,128)S(1)}, u32[]{:S(2)}, u32[]{:S(2)}) %all-to-all-start) | async-done | bytes 950304 | tf_op jit(solution)/shard_map/gather_columns/all_to_all | solution.py:273
  29.4 0.0 copy-start
  29.4 1.5 %copy-done = f32[8,224,232]{2,1,0:T(8,128)S(1)} copy-done((f32[8,224,232]{2,1,0:T(8,128)S(1)}, f32[8,224,232]{2,1,0:T(8,128)}, u32[]{:S(2)}) %copy-start) | copy-done | bytes 1663000
  30.9 0.0 copy-start.1
  30.9 1.0 %copy-done.1 = f32[1,128,1024]{2,1,0:T(8,128)S(1)} copy-done((f32[1,128,1024]{2,1,0:T(8,128)S(1)}, f32[1,128,1024]{2,1,0:T(8,128)}, u32[]{:S(2)}) %copy-start.1) | copy-done | bytes 524312
  31.9 0.0 copy-start.2
  31.9 1.0 %copy-done.2 = f32[1,128,1024]{2,1,0:T(8,128)S(1)} copy-done((f32[1,128,1024]{2,1,0:T(8,128)S(1)}, f32[1,128,1024]{2,1,0:T(8,128)}, u32[]{:S(2)}) %copy-start.2) | copy-done | bytes 524312
  33.0 10.0 %wavelet_update.1 = (f32[1,128,1024]{2,1,0:T(8,128)}, f32[8,232,128]{2,1,0:T(8,128)S(1)}) custom-call(s32[1]{0:T(128)} %bitcast.basis_ref, f32[8,232,128]{2,1,0:T(8,128)S(1)} %all-to-all-done.image_ref, f32[1,128,1024]{2,1,0:T(8,128)S(1)} %copy-done.1, f32[1,128,1024]{2,1,0:T(8,128)S(1)} %copy-done.2, f32[8,224,232]{2,1,0:T(8,128)S(1)} %copy-done, ...), custom_call_target="tpu_custom_call" | custom-call | tf_op jit(solution)/shard_map/wavelet_update/pallas_call | solution.py:248
  43.0 20.6 %all_to_all.10 = f32[8,232,128]{2,1,0:T(8,128)S(1)} all-to-all(f32[8,232,128]{2,1,0:T(8,128)S(1)} %get-tuple-element.5), channel_id=1, replica_groups=mesh['strip'=32,'basis'=8] {'basis'}, dimensions={0} | all-to-all | bytes 1900544 | tf_op jit(solution)/shard_map/sum_over_bases/all_to_all | solution.py:278
  63.7 0.1 collective-permute-start.1
  63.8 5.7 %collective-permute-done.1 = f32[104,128]{1,0:T(8,128)S(1)} collective-permute-done((f32[104,128]{1,0:T(8,128)S(1)}, f32[104,128]{1,0:T(8,128)S(1)}, u32[]{:S(2)}, u32[]{:S(2)}) %collective-permute-start.1) | collective-permute-done | bytes 53280 | tf_op jit(solution)/shard_map/rows_to_next_strip/ppermute | solution.py:263
  69.4 0.6 slice_add_fusion
  (2 shorter events, 0.1 us)
Async XLA Ops:
  1.4 2.4 %collective-permute-start = (f32[104,128]{1,0:T(8,128)S(1)}, f32[104,128]{1,0:T(8,128)S(1)}, u32[]{:S(2)}, u32[]{:S(2)}) collective-permute-start(f32[104,128]{1,0:T(8,128)S(1)} %slice.9), channel_id=1, source_target_pairs={{0,248},{8,0},{16,8},{24,16},{32,24},{40,32},{48,40},{56,48},{64,5... | collective-permute-start | bytes 159752 | tf_op jit(solution)/shard_map/rows_of_next_strip/ppermute | solution.py:263
  5.7 23.7 %all-to-all-start = ((f32[8,232,128]{2,1,0:T(8,128)}), f32[8,232,128]{2,1,0:T(8,128)S(1)}, u32[]{:S(2)}, u32[]{:S(2)}) async-start(f32[8,232,128]{2,1,0:T(8,128)} %broadcast_in_dim.3), calls=%async_computation | async-start | bytes 1900544 | tf_op jit(solution)/shard_map/gather_columns/all_to_all | solution.py:273
  29.4 1.5 %copy-start = (f32[8,224,232]{2,1,0:T(8,128)S(1)}, f32[8,224,232]{2,1,0:T(8,128)}, u32[]{:S(2)}) copy-start(f32[8,224,232]{2,1,0:T(8,128)} %constant.12.clone.rows_ref) | copy-start | bytes 4988932
  30.9 1.0 %copy-start.1 = (f32[1,128,1024]{2,1,0:T(8,128)S(1)}, f32[1,128,1024]{2,1,0:T(8,128)}, u32[]{:S(2)}) copy-start(f32[1,128,1024]{2,1,0:T(8,128)} %dual_ref.1) | copy-start | bytes 1572868
  31.9 1.0 %copy-start.2 = (f32[1,128,1024]{2,1,0:T(8,128)S(1)}, f32[1,128,1024]{2,1,0:T(8,128)}, u32[]{:S(2)}) copy-start(f32[1,128,1024]{2,1,0:T(8,128)} %limit_ref.1) | copy-start | bytes 1572868
  63.7 5.7 %collective-permute-start.1 = (f32[104,128]{1,0:T(8,128)S(1)}, f32[104,128]{1,0:T(8,128)S(1)}, u32[]{:S(2)}, u32[]{:S(2)}) collective-permute-start(f32[104,128]{1,0:T(8,128)S(1)} %slice.13), channel_id=1, source_target_pairs={{0,8},{8,16},{16,24},{24,32},{32,40},{40,48},{48,56},{56,64},{64,7... | collective-permute-start | bytes 159752 | tf_op jit(solution)/shard_map/rows_to_next_strip/ppermute | solution.py:263
where the time goes:
time: 70.5 us; the launch traced here: 70.1 us
  waiting for transfers between devices  24.5 us (35%)
  blocking collectives  20.6 us (29%)
  Pallas kernels  10 us (14%)
  starting transfers between devices  7.28 us (10%)
  local copies, waits for them, and re-layouts  5.42 us (8%)
  other arithmetic  1.53 us (2%)
    all_to_all x1, blocking collectives, on_device(): summed = jnp.sum(lax.all_to_all(adjoint, 'basis', 0, 0), axis=0)  20.6 us
    all_to_all x1, waiting for transfers between devices, on_device(): lax.all_to_all(jnp.broadcast_to(block, (BASES, EXT, 128)), 'basis', 0, 0)  17.1 us
    pallas_call x1, Pallas kernels, wavelet_update(): pl.pallas_call(wavelet_kernel, grid_spec=grid_spec, out_shape=(jax.ShapeD...  10 us
    ppermute x2, waiting for transfers between devices, shifted(): return lax.ppermute(value, 'strip', pairs)  7.45 us
    all_to_all x1, starting transfers between devices, on_device(): lax.all_to_all(jnp.broadcast_to(block, (BASES, EXT, 128)), 'basis', 0, 0)  6.64 us
    unnamed x6, local copies, waits for them, and re-layouts  3.58 us
  transfers between devices with their start and end apart: 3, of which 3 were waited for; matrix products, arithmetic and copies ran while one was open for 0% of the time, Pallas kernels for 0%

commit v1 on v0

v1 whole, which is shorter than its diff:
```python
import math

import jax
import jax.numpy as jnp
import ml_dtypes
import numpy as np
from jax import lax
from jax.experimental import pallas as pl
from jax.experimental.pallas import tpu as pltpu
from jax.sharding import PartitionSpec as P

BASES = 8
ROWS = 128
COLS = 1024
TILE = 256
TILES = COLS // TILE
BANDS = 224


daubechies = [
    [0.7071067811865476, 0.7071067811865476],
    [0.48296291314469025, 0.836516303737469, 0.22414386804185735, -0.12940952255092145],
    [
        0.3326705529509569,
        0.8068915093133388,
        0.4598775021193313,
        -0.13501102001039084,
        -0.08544127388224149,
        0.035226291882100656,
    ],
    [
        0.23037781330885523,
        0.7148465705525415,
        0.6308807679295904,
        -0.02798376941698385,
        -0.18703481171888114,
        0.030841381835986965,
        0.032883011666982945,
        -0.010597401784997278,
    ],
    [
        0.160102397974125,
        0.6038292697974729,
        0.7243085284385744,
        0.13842814590110342,
        -0.24229488706619015,
        -0.03224486958502952,
        0.07757149384006515,
        -0.006241490213011705,
        -0.012580751999015526,
        0.003335725285001549,
    ],
    [
        0.11154074335008017,
        0.4946238903983854,
        0.7511339080215775,
        0.3152503517092432,
        -0.22626469396516913,
        -0.12976686756709563,
        0.09750160558707936,
        0.02752286553001629,
        -0.031582039318031156,
        0.0005538422009938016,
        0.004777257511010651,
        -0.00107730108499558,
    ],
    [
        0.07785205408506236,
        0.39653931948230575,
        0.7291320908465551,
        0.4697822874053586,
        -0.14390600392910627,
        -0.22403618499416572,
        0.07130921926705004,
        0.08061260915106681,
        -0.03802993693503463,
        -0.01657454163101562,
        0.012550998556013784,
        0.00042957797300470274,
        -0.0018016407039998328,
        0.0003537138000010399,
    ],
    [
        0.05441584224308161,
        0.3128715909144659,
        0.6756307362980128,
        0.5853546836548691,
        -0.015829105256023893,
        -0.2840155429624281,
        0.00047248457399797254,
        0.128747426620186,
        -0.01736930100202211,
        -0.04408825393106472,
        0.013981027917015516,
        0.008746094047015655,
        -0.00487035299301066,
        -0.0003917403729959771,
        0.0006754494059985568,
        -0.00011747678400228192,
    ],
]


def composed_filters():
    filters = []
    for taps in daubechies:
        length = len(taps)
        low = np.zeros(16)
        high = np.zeros(16)
        low[:length] = np.float32(taps)
        high[:length] = [(-1) ** k * np.float32(taps[length - 1 - k]) for k in range(length)]
        levels = [(low, high)]
        for level in (1, 2):
            coarse = levels[-1][0]
            step = 2**level
            pair = []
            for band in (low, high):
                longer = np.zeros(len(coarse) + 15 * step)
                for k in range(16):
                    longer[k * step : k * step + len(coarse)] += band[k] * coarse
                pair.append(longer)
            levels.append(tuple(pair))
        filters.append(levels)
    return filters


def own_bands():
    odd = [(1, r) for r in range(1, ROWS, 2)]
    even = [(1, r) for r in range(0, ROWS, 2)]
    return odd + even + [(2, r) for r in range(0, ROWS, 2)] + [(3, r) for r in range(0, ROWS, 4)]


def rim_bands():
    first = [(1, r) for r in range(113, ROWS, 2)] + [(1, r) for r in range(112, ROWS, 2)]
    second = [(2, r) for start, step in ((80, 4), (82, 4), (112, 2)) for r in range(start, start + 8 * step, step)]
    third = [(3, r) for start in (16, 48, 80) for r in range(start, start + 32, 4)]
    return first + second + [None] * 8 + third + [(3, r) if r % 4 == 0 else None for r in range(112, ROWS, 2)]


def row_operator(levels, bands):
    rows = np.zeros((len(bands), 2 * ROWS))
    for at, band in enumerate(bands):
        if band is not None:
            level, row = band
            half = 2 ** (level - 1)
            taps = levels[level - 1][(row // half) % 2]
            start = row - row % (2 * half)
            rows[at, start : start + len(taps)] = taps / math.sqrt(BASES)
    return rows


def column_operators(levels):
    columns = np.zeros((3, TILE + 128, TILE))
    for level in (1, 2, 3):
        half = 2 ** (level - 1)
        for column in range(0, TILE, half):
            taps = levels[level - 1][(column // half) % 2]
            start = column - column % (2 * half)
            columns[level - 1, start : start + len(taps), column] = taps
    return columns


def two_parts(matrix):
    high = matrix.astype(ml_dtypes.bfloat16)
    low = (matrix - high.astype(np.float64)).astype(ml_dtypes.bfloat16)
    return np.stack([high, low], axis=1)


def operators():
    filters = composed_filters()
    own = np.stack([row_operator(levels, own_bands())[:, :ROWS] for levels in filters])
    rim = np.stack([row_operator(levels, rim_bands())[:, ROWS:] for levels in filters])
    columns = np.stack([column_operators(levels) for levels in filters])
    back = np.concatenate([columns[:, :, TILE:, 128:].transpose(0, 1, 3, 2), np.zeros((BASES, 3, 128, 128))], axis=3)
    columns_back = np.concatenate([back, columns[:, :, :TILE, :].transpose(0, 1, 3, 2)], axis=2)
    return [
        two_parts(m)
        for m in (np.concatenate([rim, own], axis=1), columns, columns_back, own.transpose(0, 2, 1), rim.transpose(0, 2, 1))
    ]


def split(value):
    high = value.astype(jnp.bfloat16)
    return high, (value - high.astype(jnp.float32)).astype(jnp.bfloat16)


def product(a, b):
    dot = lambda p, q: jnp.dot(p, q, preferred_element_type=jnp.float32)
    return dot(a[0], b[0]) + (dot(a[0], b[1]) + dot(a[1], b[0]))


def column_product(refs, spans, matrix_ref):
    results = []
    for level, (first, last) in enumerate(spans):
        stacked = tuple(
            jnp.concatenate([ref[first:last, t * TILE : (t + 1) * TILE + 128] for t in range(TILES)], axis=0)
            for ref in refs
        )
        out = product(stacked, (matrix_ref[0, level], matrix_ref[1, level]))
        count = last - first
        results.append([out[t * count : (t + 1) * count] for t in range(TILES)])
    return list(zip(*results))


OWN_SPANS = ((0, 128), (128, 192), (192, 224))
RIM_SPANS = ((0, 16), (16, 48), (48, 80))


def lane_masks(rows):
    column = lax.broadcasted_iota(jnp.int32, (rows, 128), 1)
    row = lax.broadcasted_iota(jnp.int32, (rows, 128), 0)
    fourth = column % 4 == 0
    return column % 2 == 0, fourth, jnp.logical_and(fourth, row % 2 == 0)


def pack(first, second, even):
    return jnp.where(even, first, pltpu.roll(second, 1, 1))


def unpack_second(packed):
    return pltpu.roll(packed, 127, 1)


def join(tiles, t):
    return jnp.concatenate([tiles[2 * t], tiles[2 * t + 1]], axis=1)


def rows_kernel(image_ref, rows_ref, columns_ref, send_ref, high_ref, low_ref, rim_high, rim_low):
    row_op = (rows_ref[0], rows_ref[1])
    for t in range(TILES):
        at = slice(t * TILE, (t + 1) * TILE)
        bands = product(row_op, split(join(image_ref, t)))
        for ref, part in zip((rim_high, rim_low, high_ref, low_ref), split(bands[:80]) + split(bands[80:])):
            ref[:, at] = part
            if t == 0:
                ref[:, COLS:] = part[:, :128]
    even, fourth, third = lane_masks(8)
    for t, (one, two, three) in enumerate(column_product((rim_high, rim_low), RIM_SPANS, columns_ref)):
        for h in range(2):
            lanes = slice(128 * h, 128 * h + 128)
            a, b, c = one[:, lanes], two[:, lanes], three[:, lanes]
            send = send_ref.at[2 * t + h]
            send[0:8] = a[0:8]
            send[8:16] = jnp.where(even, jnp.where(third, c[24:32], b[16:24]), a[8:16])
            send[16:24] = pack(jnp.where(fourth, c[16:24], b[0:8]), b[8:16], even)
            send[24:32] = pack(c[0:8], c[8:16], even)


def own_coefficients_kernel(high_ref, low_ref, columns_ref, dual_ref, base_ref):
    even, _, _ = lane_masks(64)
    _, fourth, _ = lane_masks(32)
    for t, (one, two, three) in enumerate(column_product((high_ref, low_ref), OWN_SPANS, columns_ref)):
        for h in range(2):
            lanes = slice(128 * h, 128 * h + 128)
            field = base_ref.at[2 * t + h]
            field[pl.ds(1, 64, 2), :] = one[:64, lanes]
            field[pl.ds(0, 64, 2), :] = jnp.where(even, two[:, lanes], one[64:, lanes])
            field[pl.ds(0, 32, 4), :] = jnp.where(fourth, three[:, lanes], field[pl.ds(0, 32, 4), :])
            field[...] += dual_ref[0, :, t * TILE + 128 * h : t * TILE + 128 * h + 128]


def update_kernel(base_ref, rim_ref, limit_ref, fresh_ref, send_ref):
    even, _, _ = lane_masks(8)
    for b in range(8):
        field, rim, send = fresh_ref.at[b], rim_ref.at[b], send_ref.at[b]
        field[...] = base_ref[b]
        second, third = rim[16:24], rim[24:32]
        field[pl.ds(113, 8, 2), :] += rim[0:8]
        field[pl.ds(112, 8, 2), :] += rim[8:16]
        for start, packed in ((80, second), (16, third)):
            later = start + (2 if start == 80 else 32)
            field[pl.ds(start, 8, 4), :] += jnp.where(even, packed, 0.0)
            field[pl.ds(later, 8, 4), :] += jnp.where(even, unpack_second(packed), 0.0)
        limit = limit_ref[0, :, 128 * b : 128 * b + 128]
        field[...] = jnp.minimum(jnp.maximum(field[...], -limit), limit)
        send[0:8] = field[pl.ds(113, 8, 2), :]
        send[8:16] = field[pl.ds(112, 8, 2), :]
        send[16:24] = pack(field[pl.ds(80, 8, 4), :], field[pl.ds(82, 8, 4), :], even)
        send[24:32] = pack(field[pl.ds(16, 8, 4), :], field[pl.ds(48, 8, 4), :], even)


def own_rows_kernel(fresh_ref, back_ref, rows_back_ref, next_ref, out_ref, high, low):
    even, _, third = lane_masks(64)
    for b in range(8):
        field = fresh_ref.at[b]
        next_ref[0, :, 128 * b : 128 * b + 128] = field[...]
        odd_rows, even_rows, coarse = field[pl.ds(1, 64, 2), :], field[pl.ds(0, 64, 2), :], field[pl.ds(0, 32, 4), :]
        parts = split(
            jnp.concatenate(
                [odd_rows, jnp.where(even, 0.0, even_rows), jnp.where(third, 0.0, even_rows), coarse], axis=0
            )
        )
        for ref, part in zip((high, low), parts):
            ref[:, 128 * b + 128 : 128 * b + 256] = part
            if b == 7:
                ref[:, 0:128] = part
    row_op = (rows_back_ref[0], rows_back_ref[1])
    for t, bands in enumerate(column_product((high, low), OWN_SPANS, back_ref)):
        part = product(row_op, split(jnp.concatenate(bands, axis=0)))
        out_ref[2 * t] = part[:, :128]
        out_ref[2 * t + 1] = part[:, 128:]


def rim_rows_kernel(own_ref, rim_ref, back_ref, rows_rim_ref, out_ref, high, low):
    even, fourth, third = lane_masks(8)
    for b in range(8):
        rim = rim_ref.at[b]
        odd_rows, even_rows, second, coarse = rim[0:8], rim[8:16], rim[16:24], rim[24:32]
        parts = split(
            jnp.concatenate(
                [
                    odd_rows,
                    jnp.where(even, 0.0, even_rows),
                    jnp.where(fourth, 0.0, second),
                    unpack_second(second),
                    jnp.where(third, 0.0, even_rows),
                    jnp.zeros_like(coarse),
                    coarse,
                    unpack_second(coarse),
                    second,
                    even_rows,
                ],
                axis=0,
            )
        )
        for ref, part in zip((high, low), parts):
            ref[:, 128 * b + 128 : 128 * b + 256] = part
            if b == 7:
                ref[:, 0:128] = part
    row_op = (rows_rim_ref[0], rows_rim_ref[1])
    for t, bands in enumerate(column_product((high, low), RIM_SPANS, back_ref)):
        part = product(row_op, split(jnp.concatenate(bands, axis=0)))
        out_ref[2 * t] = own_ref[2 * t] + part[:, :128]
        out_ref[2 * t + 1] = own_ref[2 * t + 1] + part[:, 128:]


F32, BF16 = jnp.float32, jnp.bfloat16
FIELD = ((BASES, ROWS, 128), F32)
RIM = ((BASES, 32, 128), F32)
WOVEN = ((1, ROWS, COLS), F32)
WIDE = ((BANDS, COLS + 128), BF16)


def call(kernel, name, out_shape, *operands, scratch=()):
    vmem = pl.BlockSpec(memory_space=pltpu.VMEM)
    return pl.pallas_call(
        kernel,
        in_specs=[vmem] * len(operands),
        out_specs=tuple(vmem for _ in out_shape),
        out_shape=tuple(jax.ShapeDtypeStruct(*o) for o in out_shape),
        scratch_shapes=[pltpu.VMEM(*s) for s in scratch],
        compiler_params=pltpu.CompilerParams(vmem_limit_bytes=32 * 1024 * 1024),
        name=name,
    )(*operands)


def shifted(value, steps):
    count = lax.axis_size("strip")
    pairs = [(source, (source + steps) % count) for source in range(count)]
    return lax.ppermute(value, "strip", pairs)


def local_update(field, dual_coeffs, thresholds, matrices, shift):
    rows, columns, columns_back, rows_back, rows_rim = matrices
    rim_scratch = ((80, COLS + 128), BF16)
    rim, high, low = call(
        rows_kernel, "row_bands", (RIM, WIDE, WIDE), field, rows, columns, scratch=(rim_scratch, rim_scratch)
    )
    with jax.named_scope("rim_coefficients"):
        rim = shift(rim, -1)
    (base,) = call(own_coefficients_kernel, "own_coefficients", (FIELD,), high, low, columns, dual_coeffs)
    fresh, rim = call(update_kernel, "clip_update", (FIELD, RIM), base, rim, thresholds)
    with jax.named_scope("rim_of_update"):
        rim = shift(rim, 1)
    dual_next, own = call(
        own_rows_kernel, "own_rows", (WOVEN, FIELD), fresh, columns_back, rows_back, scratch=(WIDE, WIDE)
    )
    (whole,) = call(
        rim_rows_kernel, "rim_rows", (FIELD,), own, rim, columns_back, rows_rim, scratch=(rim_scratch, rim_scratch)
    )
    return dual_next, whole


def on_device(sky_image, dual_coeffs, thresholds):
    basis = lax.axis_index("basis")
    matrices = [lax.dynamic_index_in_dim(jnp.asarray(m), basis, 0, False) for m in operators()]
    with jax.named_scope("gather_columns"):
        field = lax.all_to_all(jnp.broadcast_to(sky_image, (BASES, ROWS, 128)), "basis", 0, 0)
        field, *matrices = lax.optimization_barrier((field, *matrices))
    dual_next, whole = local_update(field, dual_coeffs, thresholds, matrices, shifted)
    with jax.named_scope("sum_over_bases"):
        adjoint_image = jnp.sum(lax.all_to_all(whole, "basis", 0, 0), axis=0)
    return (dual_next, adjoint_image)


def solution(mesh):
    placed = (P("strip", "basis"), P("basis", "strip", None), P("basis", "strip", None))
    return jax.shard_map(
        on_device,
        mesh=mesh,
        in_specs=placed,
        out_specs=(P("basis", "strip", None), P("strip", "basis")),
        check_vma=False,
    )
```

time: 70.5 us -> 50.3 us (0.71)
  the two profiles are of different devices: /device:TPU:128 before, /device:TPU:2 now
where the time goes in v1:
time: 50.3 us; the launch traced here: 50 us
  blocking collectives  14.6 us (29%)
  starting transfers between devices  11.3 us (22%)
  waiting for transfers between devices  11.3 us (22%)
  local copies, waits for them, and re-layouts  6.15 us (12%)
  Pallas kernels  5.39 us (11%)
  between operations  0.67 us (1%)
  other arithmetic  0.66 us (1%)
    all_to_all x1, blocking collectives, on_device(): adjoint_image = jnp.sum(lax.all_to_all(whole, 'basis', 0, 0), axis=0)  14.6 us
    all_to_all x1, starting transfers between devices, on_device(): lax.all_to_all(jnp.broadcast_to(sky_image, (BASES, ROWS, 128)), 'basis',...  7.46 us
    ppermute x2, waiting for transfers between devices, shifted(): return lax.ppermute(value, 'strip', pairs)  6.13 us
    pallas_call x5, Pallas kernels, call(): pl.pallas_call(kernel, in_specs=[vmem] * len(operands), out_specs=tuple((...  5.39 us
    all_to_all x1, waiting for transfers between devices, on_device(): lax.all_to_all(jnp.broadcast_to(sky_image, (BASES, ROWS, 128)), 'basis',...  5.13 us
    squeeze x4, local copies, waits for them, and re-layouts, on_device(): lax.dynamic_index_in_dim(jnp.asarray(m), basis, 0, False)  4.47 us
    ppermute x2, starting transfers between devices, shifted(): return lax.ppermute(value, 'strip', pairs)  3.8 us
    broadcast_in_dim x1, local copies, waits for them, and re-layouts, on_device(): jnp.broadcast_to(sky_image, (BASES, ROWS, 128))  1.67 us
  transfers between devices with their start and end apart: 3, of which 3 were waited for; matrix products, arithmetic and copies ran while one was open for 9% of the time, Pallas kernels for 6%

profile of v1, /device:TPU:2, one launch (start us, length us, event | category | flops | bytes accessed | tf_op | source)
XLA Modules:
  0.0 50.0 jit_solution(7435424799419055445)
XLA Ops:
  0.6 1.7 %broadcast_in_dim.3 = f32[8,128,128]{2,1,0:T(8,128)} broadcast(f32[128,128]{1,0:T(8,128)} %param.8), dimensions={1,2} | broadcast | bytes 589824 | tf_op jit(solution)/shard_map/gather_columns/broadcast_in_dim | solution.py:388
  2.3 7.5 %all-to-all-start = ((f32[8,128,128]{2,1,0:T(8,128)}), f32[8,128,128]{2,1,0:T(8,128)S(1)}, u32[]{:S(2)}, u32[]{:S(2)}) async-start(f32[8,128,128]{2,1,0:T(8,128)} %broadcast_in_dim.3), calls=%async_computation | async-start | bytes 1048576 | tf_op jit(solution)/shard_map/gather_columns/all_to_all | solution.py:388
  9.8 0.8 %dynamic-slice_bitcast_fusion.4.rows_rim_ref = bf16[2,128,80]{2,1,0:T(8,128)(2,1)S(1)} fusion(bf16[8,2,128,80]{3,2,1,0:T(8,128)(2,1)} %constant.40.clone, s32[]{:T(128)S(6)} %select_n.11), kind=kLoop, calls=%fused_computation.4 | loop fusion | bytes 81924 | tf_op jit(solution)/shard_map/jit(dynamic_index_in_dim)/squeeze | solution.py:386
  10.6 0.9 %dynamic-slice_bitcast_fusion.3.rows_back_ref = bf16[2,128,224]{2,1,0:T(8,128)(2,1)S(1)} fusion(bf16[8,2,128,224]{3,2,1,0:T(8,128)(2,1)} %constant.39.clone, s32[]{:T(128)S(6)} %select_n.11), kind=kLoop, calls=%fused_computation.3 | loop fusion | bytes 229380 | tf_op jit(solution)/shard_map/jit(dynamic_index_in_dim)/squeeze | solution.py:386
  11.5 0.9 %dynamic-slice_bitcast_fusion.2.rows_ref = bf16[2,304,128]{2,1,0:T(8,128)(2,1)S(1)} fusion(bf16[8,2,304,128]{3,2,1,0:T(8,128)(2,1)} %constant.36.clone, s32[]{:T(128)S(6)} %select_n.11), kind=kLoop, calls=%fused_computation.2 | loop fusion | bytes 311300 | tf_op jit(solution)/shard_map/jit(dynamic_index_in_dim)/squeeze | solution.py:386
  12.5 1.8 %dynamic-slice_bitcast_fusion = (bf16[2,3,384,256]{3,2,1,0:T(8,128)(2,1)S(1)}, bf16[2,3,384,256]{3,2,1,0:T(8,128)(2,1)S(1)}) fusion(bf16[8,2,3,384,256]{4,3,2,1,0:T(8,128)(2,1)} %constant.38.clone, s32[]{:T(128)S(6)} %select_n.11, bf16[8,2,3,384,256]{4,3,2,1,0:T(8,128)(2,1)} %constant.37.clone), kind=kLoop, calls=%fused_computation | loop fusion | bytes 4718596 | tf_op jit(solution)/shard_map/jit(dynamic_index_in_dim)/squeeze | solution.py:386
  14.2 5.1 %all-to-all-done.image_ref = f32[8,128,128]{2,1,0:T(8,128)S(1)} async-done(((f32[8,128,128]{2,1,0:T(8,128)}), f32[8,128,128]{2,1,0:T(8,128)S(1)}, u32[]{:S(2)}, u32[]{:S(2)}) %all-to-all-start) | async-done | bytes 524320 | tf_op jit(solution)/shard_map/gather_columns/all_to_all | solution.py:388
  19.4 0.0 copy-start
  19.4 1.2 %row_bands.1 = (f32[8,32,128]{2,1,0:T(8,128)S(1)}, bf16[224,1152]{1,0:T(8,128)(2,1)S(1)}, bf16[224,1152]{1,0:T(8,128)(2,1)S(1)}) custom-call(f32[8,128,128]{2,1,0:T(8,128)S(1)} %all-to-all-done.image_ref, bf16[2,304,128]{2,1,0:T(8,128)(2,1)S(1)} %dynamic-slice_bitcast_fusion.2.rows_ref, bf16[2,3,384,256]{3,2,1,0:T(8,128)(2,1)S(1)} %get-tuple-element.17.columns_ref), custom_call_target="tpu_custom_call" | custom-call | tf_op jit(solution)/shard_map/row_bands/pallas_call | solution.py:346
  20.6 3.7 %collective-permute-start = (f32[8,32,128]{2,1,0:T(8,128)S(1)}, f32[8,32,128]{2,1,0:T(8,128)S(1)}, u32[]{:S(2)}, u32[]{:S(2)}) collective-permute-start(f32[8,32,128]{2,1,0:T(8,128)S(1)} %get-tuple-element.20), channel_id=1, source_target_pairs={{0,248},{8,0},{16,8},{24,16},{32,24},{40,32},{48,40},{56,48},{64,5... | collective-permute-start | bytes 393224 | tf_op jit(solution)/shard_map/rim_coefficients/ppermute | solution.py:360
  24.3 0.0 copy-done
  24.3 0.0 copy-start.1
  24.3 0.9 %own_coefficients.1.base_ref = f32[8,128,128]{2,1,0:T(8,128)S(1)} custom-call(bf16[224,1152]{1,0:T(8,128)(2,1)S(1)} %get-tuple-element.18.high_ref, bf16[224,1152]{1,0:T(8,128)(2,1)S(1)} %get-tuple-element.19.low_ref, bf16[2,3,384,256]{3,2,1,0:T(8,128)(2,1)S(1)} %get-tuple-element.17.columns_ref, f32[1,128,1024]{2,1,0:T(8,128)S(1)} %copy-done), custom_call_target="tpu_custom_call" | custom-call | tf_op jit(solution)/shard_map/own_coefficients/pallas_call | solution.py:346
  25.2 1.6 %collective-permute-done.rim_ref = f32[8,32,128]{2,1,0:T(8,128)S(1)} collective-permute-done((f32[8,32,128]{2,1,0:T(8,128)S(1)}, f32[8,32,128]{2,1,0:T(8,128)S(1)}, u32[]{:S(2)}, u32[]{:S(2)}) %collective-permute-start) | collective-permute-done | bytes 131104 | tf_op jit(solution)/shard_map/rim_coefficients/ppermute | solution.py:360
  26.8 0.0 copy-done.1
  26.8 0.2 clip_update.1
  27.1 0.1 collective-permute-start.1
  27.1 2.1 %own_rows.1 = (f32[1,128,1024]{2,1,0:T(8,128)}, f32[8,128,128]{2,1,0:T(8,128)S(1)}) custom-call(f32[8,128,128]{2,1,0:T(8,128)S(1)} %get-tuple-element.21.fresh_ref, bf16[2,3,384,256]{3,2,1,0:T(8,128)(2,1)S(1)} %get-tuple-element.22.back_ref, bf16[2,128,224]{2,1,0:T(8,128)(2,1)S(1)} %dynamic-slice_bitcast_fusion.3.rows_back_ref), custom_call_target="tpu_custom_call" | custom-call | tf_op jit(solution)/shard_map/own_rows/pallas_call | solution.py:346
  29.2 4.5 %collective-permute-done.1.rim_ref = f32[8,32,128]{2,1,0:T(8,128)S(1)} collective-permute-done((f32[8,32,128]{2,1,0:T(8,128)S(1)}, f32[8,32,128]{2,1,0:T(8,128)S(1)}, u32[]{:S(2)}, u32[]{:S(2)}) %collective-permute-start.1) | collective-permute-done | bytes 131104 | tf_op jit(solution)/shard_map/rim_of_update/ppermute | solution.py:360
  33.8 1.0 %rim_rows.1 = f32[8,128,128]{2,1,0:T(8,128)S(1)} custom-call(f32[8,128,128]{2,1,0:T(8,128)S(1)} %get-tuple-element.25.own_ref, f32[8,32,128]{2,1,0:T(8,128)S(1)} %collective-permute-done.1.rim_ref, bf16[2,3,384,256]{3,2,1,0:T(8,128)(2,1)S(1)} %get-tuple-element.22.back_ref, bf16[2,128,80]{2,1,0:T(8,128)(2,1)S(1)} %dynamic-slice_bitcast_fusion.4.rows_rim_ref), custom_call_target="tpu_custom_call" | custom-call | tf_op jit(solution)/shard_map/rim_rows/pallas_call | solution.py:346
  34.7 14.6 %all_to_all.10 = f32[8,128,128]{2,1,0:T(8,128)S(1)} all-to-all(f32[8,128,128]{2,1,0:T(8,128)S(1)} %rim_rows.1), channel_id=1, replica_groups=mesh['strip'=32,'basis'=8] {'basis'}, dimensions={0} | all-to-all | bytes 1048576 | tf_op jit(solution)/shard_map/sum_over_bases/all_to_all | solution.py:392
  49.3 0.7 %reduce_sum.9 = f32[128,128]{1,0:T(8,128)} reduce(f32[8,128,128]{2,1,0:T(8,128)S(1)} %all_to_all.10, f32[]{:T(128)} %constant.35.clone.1), dimensions={0}, to_apply=%region_0.1 | reduce | flops 114688 | bytes 589828 | tf_op jit(solution)/shard_map/sum_over_bases/reduce_sum | solution.py:392
Async XLA Ops:
  2.3 17.1 %all-to-all-start = ((f32[8,128,128]{2,1,0:T(8,128)}), f32[8,128,128]{2,1,0:T(8,128)S(1)}, u32[]{:S(2)}, u32[]{:S(2)}) async-start(f32[8,128,128]{2,1,0:T(8,128)} %broadcast_in_dim.3), calls=%async_computation | async-start | bytes 1048576 | tf_op jit(solution)/shard_map/gather_columns/all_to_all | solution.py:388
  19.4 4.9 %copy-start = (f32[1,128,1024]{2,1,0:T(8,128)S(1)}, f32[1,128,1024]{2,1,0:T(8,128)}, u32[]{:S(2)}) copy-start(f32[1,128,1024]{2,1,0:T(8,128)} %dual_ref.1) | copy-start | bytes 1572868
  20.6 6.3 %collective-permute-start = (f32[8,32,128]{2,1,0:T(8,128)S(1)}, f32[8,32,128]{2,1,0:T(8,128)S(1)}, u32[]{:S(2)}, u32[]{:S(2)}) collective-permute-start(f32[8,32,128]{2,1,0:T(8,128)S(1)} %get-tuple-element.20), channel_id=1, source_target_pairs={{0,248},{8,0},{16,8},{24,16},{32,24},{40,32},{48,40},{56,48},{64,5... | collective-permute-start | bytes 393224 | tf_op jit(solution)/shard_map/rim_coefficients/ppermute | solution.py:360
  24.3 2.5 %copy-start.1 = (f32[1,128,1024]{2,1,0:T(8,128)S(1)}, f32[1,128,1024]{2,1,0:T(8,128)}, u32[]{:S(2)}) copy-start(f32[1,128,1024]{2,1,0:T(8,128)} %limit_ref.1) | copy-start | bytes 1572868
  27.1 6.7 %collective-permute-start.1 = (f32[8,32,128]{2,1,0:T(8,128)S(1)}, f32[8,32,128]{2,1,0:T(8,128)S(1)}, u32[]{:S(2)}, u32[]{:S(2)}) collective-permute-start(f32[8,32,128]{2,1,0:T(8,128)S(1)} %get-tuple-element.26), channel_id=1, source_target_pairs={{0,8},{8,16},{16,24},{24,32},{32,40},{40,48},{48,56},{56,64},{64,7... | collective-permute-start | bytes 393224 | tf_op jit(solution)/shard_map/rim_of_update/ppermute | solution.py:360

commit v2 on v1

--- a/solution.py
+++ b/solution.py
@@ -1,3 +1,4 @@
+import functools
 import math
 
 import jax
@@ -150,10 +151,10 @@
 
 
 def column_operators(levels):
-    columns = np.zeros((3, TILE + 128, TILE))
+    columns = np.zeros((3, 256, 128))
     for level in (1, 2, 3):
         half = 2 ** (level - 1)
-        for column in range(0, TILE, half):
+        for column in range(0, 128, half):
             taps = levels[level - 1][(column // half) % 2]
             start = column - column % (2 * half)
             columns[level - 1, start : start + len(taps), column] = taps
@@ -162,20 +163,28 @@
 
 def two_parts(matrix):
     high = matrix.astype(ml_dtypes.bfloat16)
-    low = (matrix - high.astype(np.float64)).astype(ml_dtypes.bfloat16)
-    return np.stack([high, low], axis=1)
+    return high, (matrix - high.astype(np.float64)).astype(ml_dtypes.bfloat16)
 
 
 def operators():
     filters = composed_filters()
     own = np.stack([row_operator(levels, own_bands())[:, :ROWS] for levels in filters])
-    rim = np.stack([row_operator(levels, rim_bands())[:, ROWS:] for levels in filters])
+    rims = [row_operator(levels, rim_bands()) for levels in filters]
+    before = np.stack([m[:, ROWS:] for m in rims])
+    rim = np.stack([m[:, :ROWS] for m in rims])
     columns = np.stack([column_operators(levels) for levels in filters])
-    back = np.concatenate([columns[:, :, TILE:, 128:].transpose(0, 1, 3, 2), np.zeros((BASES, 3, 128, 128))], axis=3)
-    columns_back = np.concatenate([back, columns[:, :, :TILE, :].transpose(0, 1, 3, 2)], axis=2)
+    columns_back = np.concatenate([columns[:, :, 128:].transpose(0, 1, 3, 2), columns[:, :, :128].transpose(0, 1, 3, 2)], axis=2)
+    rows = np.concatenate([before, own, rim], axis=1)
+    gap = np.zeros((BASES, ROWS, 96))
+    own_back, before_back, rim_back = (m.transpose(0, 2, 1) for m in (own, before, rim))
+    rows_back = np.concatenate(
+        [own_back, gap[:, :, :32], before_back, before_back, gap, rim_back, rim_back], axis=2
+    )
     return [
-        two_parts(m)
-        for m in (np.concatenate([rim, own], axis=1), columns, columns_back, own.transpose(0, 2, 1), rim.transpose(0, 2, 1))
+        np.stack(two_parts(np.concatenate([rows, rows], axis=2)), axis=1),
+        np.concatenate(two_parts(columns), axis=3),
+        np.concatenate(two_parts(columns_back), axis=3),
+        np.stack(two_parts(rows_back), axis=1),
     ]
 
 
@@ -184,21 +193,26 @@
     return high, (value - high.astype(jnp.float32)).astype(jnp.bfloat16)
 
 
-def product(a, b):
-    dot = lambda p, q: jnp.dot(p, q, preferred_element_type=jnp.float32)
-    return dot(a[0], b[0]) + (dot(a[0], b[1]) + dot(a[1], b[0]))
+def dot(a, b):
+    return jnp.dot(a, b, preferred_element_type=jnp.float32)
+
+
+def twice_product(rows_ref, at, field):
+    stacked = jnp.concatenate([rows_ref[(0, *at)], rows_ref[(1, *at)]], axis=0)
+    out = dot(stacked, jnp.concatenate(split(field), axis=0))
+    count = out.shape[0] // 2
+    return out[:count] + out[count:]
 
 
 def column_product(refs, spans, matrix_ref):
     results = []
     for level, (first, last) in enumerate(spans):
-        stacked = tuple(
-            jnp.concatenate([ref[first:last, t * TILE : (t + 1) * TILE + 128] for t in range(TILES)], axis=0)
-            for ref in refs
-        )
-        out = product(stacked, (matrix_ref[0, level], matrix_ref[1, level]))
+        stacked = jnp.concatenate([ref[first:last, 128 * b : 128 * b + 256] for ref in refs for b in range(8)], axis=0)
+        out = dot(stacked, matrix_ref[level])
+        out = out[:, :128] + out[:, 128:]
         count = last - first
-        results.append([out[t * count : (t + 1) * count] for t in range(TILES)])
+        out = out[: 8 * count] + out[8 * count :]
+        results.append([out[b * count : (b + 1) * count] for b in range(8)])
     return list(zip(*results))
 
 
@@ -225,65 +239,72 @@
     return jnp.concatenate([tiles[2 * t], tiles[2 * t + 1]], axis=1)
 
 
-def rows_kernel(image_ref, rows_ref, columns_ref, send_ref, high_ref, low_ref, rim_high, rim_low):
-    row_op = (rows_ref[0], rows_ref[1])
+def row_product(image_ref, rows_ref, span, high_ref, low_ref):
     for t in range(TILES):
-        at = slice(t * TILE, (t + 1) * TILE)
-        bands = product(row_op, split(join(image_ref, t)))
-        for ref, part in zip((rim_high, rim_low, high_ref, low_ref), split(bands[:80]) + split(bands[80:])):
-            ref[:, at] = part
+        for ref, part in zip((high_ref, low_ref), split(twice_product(rows_ref, (span,), join(image_ref, t)))):
+            ref[:, t * TILE : (t + 1) * TILE] = part
             if t == 0:
                 ref[:, COLS:] = part[:, :128]
+
+
+def packed_rim(field, even):
+    rows = lambda start, step: field[pl.ds(start, 8, step), :]
+    parts = [rows(113, 2), rows(112, 2), pack(rows(80, 4), rows(82, 4), even), pack(rows(16, 4), rows(48, 4), even)]
+    return jnp.concatenate(parts, axis=0)
+
+
+def rim_of_arguments_kernel(dual_ref, limit_ref, send_ref, fields):
+    even, _, _ = lane_masks(8)
+    for b in range(8):
+        for i, ref in enumerate((dual_ref, limit_ref)):
+            field = fields.at[2 * b + i]
+            field[...] = ref[0, :, 128 * b : 128 * b + 128]
+            send_ref[b, 32 * i : 32 * i + 32] = packed_rim(field, even)
+
+
+def rim_coefficients_kernel(first, image_ref, rows_ref, columns_ref, send_ref, high, low):
+    row_product(image_ref, rows_ref, slice(first, first + 80), high, low)
     even, fourth, third = lane_masks(8)
-    for t, (one, two, three) in enumerate(column_product((rim_high, rim_low), RIM_SPANS, columns_ref)):
-        for h in range(2):
-            lanes = slice(128 * h, 128 * h + 128)
-            a, b, c = one[:, lanes], two[:, lanes], three[:, lanes]
-            send = send_ref.at[2 * t + h]
-            send[0:8] = a[0:8]
-            send[8:16] = jnp.where(even, jnp.where(third, c[24:32], b[16:24]), a[8:16])
-            send[16:24] = pack(jnp.where(fourth, c[16:24], b[0:8]), b[8:16], even)
-            send[24:32] = pack(c[0:8], c[8:16], even)
-
-
-def own_coefficients_kernel(high_ref, low_ref, columns_ref, dual_ref, base_ref):
+    for b, (one, two, three) in enumerate(column_product((high, low), RIM_SPANS, columns_ref)):
+        send = send_ref.at[b]
+        send[0:8] = one[0:8]
+        send[8:16] = jnp.where(even, jnp.where(third, three[24:32], two[16:24]), one[8:16])
+        send[16:24] = pack(jnp.where(fourth, three[16:24], two[0:8]), two[8:16], even)
+        send[24:32] = pack(three[0:8], three[8:16], even)
+
+
+def own_update_kernel(image_ref, rows_ref, columns_ref, dual_ref, limit_ref, fresh_ref, high, low):
+    row_product(image_ref, rows_ref, slice(80, 304), high, low)
     even, _, _ = lane_masks(64)
     _, fourth, _ = lane_masks(32)
-    for t, (one, two, three) in enumerate(column_product((high_ref, low_ref), OWN_SPANS, columns_ref)):
-        for h in range(2):
-            lanes = slice(128 * h, 128 * h + 128)
-            field = base_ref.at[2 * t + h]
-            field[pl.ds(1, 64, 2), :] = one[:64, lanes]
-            field[pl.ds(0, 64, 2), :] = jnp.where(even, two[:, lanes], one[64:, lanes])
-            field[pl.ds(0, 32, 4), :] = jnp.where(fourth, three[:, lanes], field[pl.ds(0, 32, 4), :])
-            field[...] += dual_ref[0, :, t * TILE + 128 * h : t * TILE + 128 * h + 128]
-
-
-def update_kernel(base_ref, rim_ref, limit_ref, fresh_ref, send_ref):
-    even, _, _ = lane_masks(8)
-    for b in range(8):
-        field, rim, send = fresh_ref.at[b], rim_ref.at[b], send_ref.at[b]
-        field[...] = base_ref[b]
-        second, third = rim[16:24], rim[24:32]
-        field[pl.ds(113, 8, 2), :] += rim[0:8]
-        field[pl.ds(112, 8, 2), :] += rim[8:16]
-        for start, packed in ((80, second), (16, third)):
-            later = start + (2 if start == 80 else 32)
-            field[pl.ds(start, 8, 4), :] += jnp.where(even, packed, 0.0)
-            field[pl.ds(later, 8, 4), :] += jnp.where(even, unpack_second(packed), 0.0)
-        limit = limit_ref[0, :, 128 * b : 128 * b + 128]
-        field[...] = jnp.minimum(jnp.maximum(field[...], -limit), limit)
-        send[0:8] = field[pl.ds(113, 8, 2), :]
-        send[8:16] = field[pl.ds(112, 8, 2), :]
-        send[16:24] = pack(field[pl.ds(80, 8, 4), :], field[pl.ds(82, 8, 4), :], even)
-        send[24:32] = pack(field[pl.ds(16, 8, 4), :], field[pl.ds(48, 8, 4), :], even)
-
-
-def own_rows_kernel(fresh_ref, back_ref, rows_back_ref, next_ref, out_ref, high, low):
+    for b, (one, two, three) in enumerate(column_product((high, low), OWN_SPANS, columns_ref)):
+        field = fresh_ref.at[b]
+        field[pl.ds(1, 64, 2), :] = one[:64]
+        field[pl.ds(0, 64, 2), :] = jnp.where(even, two, one[64:])
+        field[pl.ds(0, 32, 4), :] = jnp.where(fourth, three, field[pl.ds(0, 32, 4), :])
+        at = slice(128 * b, 128 * b + 128)
+        limit = limit_ref[0, :, at]
+        field[...] = jnp.minimum(jnp.maximum(dual_ref[0, :, at] + field[...], -limit), limit)
+        field[112:128] = jnp.zeros((16, 128), jnp.float32)
+        for start, mask in ((80, even), (82, even), (16, fourth), (48, fourth)):
+            field[pl.ds(start, 8, 4), :] = jnp.where(mask[:8], 0.0, field[pl.ds(start, 8, 4), :])
+
+
+def previous_rim_kernel(image_ref, rows_ref, columns_ref, arguments_ref, out_ref, high, low, partial):
+    rim_coefficients_kernel(0, image_ref, rows_ref, columns_ref, partial, high, low)
+    out_ref[:, :32] = partial[...] + arguments_ref[:, :32]
+    out_ref[:, 32:] = arguments_ref[:, 32:]
+
+
+def rim_update_kernel(rim_ref, before_ref, send_ref):
+    limit = before_ref[:, 32:]
+    send_ref[...] = jnp.minimum(jnp.maximum(before_ref[:, :32] + rim_ref[...], -limit), limit)
+
+
+def own_rows_kernel(fresh_ref, back_ref, rows_back_ref, out_ref, high, low):
     even, _, third = lane_masks(64)
     for b in range(8):
         field = fresh_ref.at[b]
-        next_ref[0, :, 128 * b : 128 * b + 128] = field[...]
         odd_rows, even_rows, coarse = field[pl.ds(1, 64, 2), :], field[pl.ds(0, 64, 2), :], field[pl.ds(0, 32, 4), :]
         parts = split(
             jnp.concatenate(
@@ -294,14 +315,17 @@
             ref[:, 128 * b + 128 : 128 * b + 256] = part
             if b == 7:
                 ref[:, 0:128] = part
-    row_op = (rows_back_ref[0], rows_back_ref[1])
-    for t, bands in enumerate(column_product((high, low), OWN_SPANS, back_ref)):
-        part = product(row_op, split(jnp.concatenate(bands, axis=0)))
+    row_op = jnp.concatenate([rows_back_ref[0, :, :BANDS], rows_back_ref[1, :, :BANDS]], axis=0)
+    tiles = [jnp.concatenate(bands, axis=0) for bands in column_product((high, low), OWN_SPANS, back_ref)]
+    for t in range(TILES):
+        first, second = split(join(tiles, t))
+        part = dot(row_op, first)
+        part = part[:ROWS] + (part[ROWS:] + dot(row_op[:ROWS], second))
         out_ref[2 * t] = part[:, :128]
         out_ref[2 * t + 1] = part[:, 128:]
 
 
-def rim_rows_kernel(own_ref, rim_ref, back_ref, rows_rim_ref, out_ref, high, low):
+def add_rim_rows(first, own_ref, rim_ref, back_ref, rows_back_ref, out_ref, high, low):
     even, fourth, third = lane_masks(8)
     for b in range(8):
         rim = rim_ref.at[b]
@@ -327,29 +351,58 @@
             ref[:, 128 * b + 128 : 128 * b + 256] = part
             if b == 7:
                 ref[:, 0:128] = part
-    row_op = (rows_rim_ref[0], rows_rim_ref[1])
-    for t, bands in enumerate(column_product((high, low), RIM_SPANS, back_ref)):
-        part = product(row_op, split(jnp.concatenate(bands, axis=0)))
+    tiles = [jnp.concatenate(bands, axis=0) for bands in column_product((high, low), RIM_SPANS, back_ref)]
+    for t in range(TILES):
+        part = twice_product(rows_back_ref, (slice(None), slice(first, first + 160)), join(tiles, t))
         out_ref[2 * t] = own_ref[2 * t] + part[:, :128]
         out_ref[2 * t + 1] = own_ref[2 * t + 1] + part[:, 128:]
+
+
+def rows_of_previous_kernel(*refs):
+    add_rim_rows(256, *refs)
+
+
+def finish_kernel(own_ref, rim_ref, fresh_ref, back_ref, rows_back_ref, next_ref, out_ref, high, low, fields, sent):
+    even, fourth, _ = lane_masks(8)
+    copies = []
+    for b in range(8):
+        field, rim = fields.at[b], rim_ref.at[b]
+        field[...] = fresh_ref[b]
+        second, third = rim[16:24], rim[24:32]
+        field[pl.ds(113, 8, 2), :] = rim[0:8]
+        field[pl.ds(112, 8, 2), :] = rim[8:16]
+        for start, mask, value in (
+            (80, even, second),
+            (82, even, unpack_second(second)),
+            (16, fourth, third),
+            (48, fourth, unpack_second(third)),
+        ):
+            field[pl.ds(start, 8, 4), :] = jnp.where(mask, value, field[pl.ds(start, 8, 4), :])
+        copies.append(pltpu.make_async_copy(field, next_ref.at[0, :, pl.ds(128 * b, 128)], sent.at[b]))
+        copies[b].start()
+    add_rim_rows(512, own_ref, rim_ref, back_ref, rows_back_ref, out_ref, high, low)
+    for copy in copies:
+        copy.wait()
 
 
 F32, BF16 = jnp.float32, jnp.bfloat16
 FIELD = ((BASES, ROWS, 128), F32)
 RIM = ((BASES, 32, 128), F32)
+RIMS = ((BASES, 64, 128), F32)
 WOVEN = ((1, ROWS, COLS), F32)
 WIDE = ((BANDS, COLS + 128), BF16)
-
-
-def call(kernel, name, out_shape, *operands, scratch=()):
+RIM_WIDE = ((80, COLS + 128), BF16)
+
+
+def call(kernel, name, out_shape, *operands, scratch=(), out_specs=None, semaphores=()):
     vmem = pl.BlockSpec(memory_space=pltpu.VMEM)
     return pl.pallas_call(
         kernel,
         in_specs=[vmem] * len(operands),
-        out_specs=tuple(vmem for _ in out_shape),
+        out_specs=out_specs or tuple(vmem for _ in out_shape),
         out_shape=tuple(jax.ShapeDtypeStruct(*o) for o in out_shape),
-        scratch_shapes=[pltpu.VMEM(*s) for s in scratch],
-        compiler_params=pltpu.CompilerParams(vmem_limit_bytes=32 * 1024 * 1024),
+        scratch_shapes=[pltpu.VMEM(*s) for s in scratch] + list(semaphores),
+        compiler_params=pltpu.CompilerParams(vmem_limit_bytes=16 * 1024 * 1024),
         name=name,
     )(*operands)
 
@@ -360,34 +413,56 @@
     return lax.ppermute(value, "strip", pairs)
 
 
-def local_update(field, dual_coeffs, thresholds, matrices, shift):
-    rows, columns, columns_back, rows_back, rows_rim = matrices
-    rim_scratch = ((80, COLS + 128), BF16)
-    rim, high, low = call(
-        rows_kernel, "row_bands", (RIM, WIDE, WIDE), field, rows, columns, scratch=(rim_scratch, rim_scratch)
+def rim_of_arguments(dual_coeffs, thresholds):
+    scratch = (((2 * BASES, ROWS, 128), F32),)
+    (packed,) = call(
+        rim_of_arguments_kernel, "rim_of_arguments", (RIMS,), dual_coeffs, thresholds, scratch=scratch
+    )
+    return packed
+
+
+def local_update(field, arguments, dual_coeffs, thresholds, matrices, shift):
+    rows, columns, columns_back, rows_back = matrices
+    (rim,) = call(
+        functools.partial(rim_coefficients_kernel, 304), "rim_coefficients", (RIM,), field, rows, columns,
+        scratch=(RIM_WIDE, RIM_WIDE),
     )
     with jax.named_scope("rim_coefficients"):
-        rim = shift(rim, -1)
-    (base,) = call(own_coefficients_kernel, "own_coefficients", (FIELD,), high, low, columns, dual_coeffs)
-    fresh, rim = call(update_kernel, "clip_update", (FIELD, RIM), base, rim, thresholds)
+        rim = shift(rim, 1)
+    (fresh,) = call(
+        own_update_kernel, "own_update", (FIELD,), field, rows, columns, dual_coeffs, thresholds, scratch=(WIDE, WIDE)
+    )
+    (own,) = call(own_rows_kernel, "own_rows", (FIELD,), fresh, columns_back, rows_back, scratch=(WIDE, WIDE))
+    (before,) = call(
+        previous_rim_kernel, "previous_rim", (RIMS,), field, rows, columns, arguments, scratch=(RIM_WIDE, RIM_WIDE, RIM)
+    )
+    rim, before, fresh, own = lax.optimization_barrier((rim, before, fresh, own))
+    (update,) = call(rim_update_kernel, "rim_update", (RIM,), rim, before)
     with jax.named_scope("rim_of_update"):
-        rim = shift(rim, 1)
-    dual_next, own = call(
-        own_rows_kernel, "own_rows", (WOVEN, FIELD), fresh, columns_back, rows_back, scratch=(WIDE, WIDE)
-    )
-    (whole,) = call(
-        rim_rows_kernel, "rim_rows", (FIELD,), own, rim, columns_back, rows_rim, scratch=(rim_scratch, rim_scratch)
-    )
-    return dual_next, whole
+        rim = shift(update, -1)
+    (own,) = call(
+        rows_of_previous_kernel, "previous_rows", (FIELD,), own, update, columns_back, rows_back, scratch=(RIM_WIDE, RIM_WIDE)
+    )
+    return call(
+        finish_kernel,
+        "finish",
+        (WOVEN, FIELD),
+        own, rim, fresh, columns_back, rows_back,
+        scratch=(RIM_WIDE, RIM_WIDE, FIELD),
+        out_specs=(pl.BlockSpec(memory_space=pl.ANY), pl.BlockSpec(memory_space=pltpu.VMEM)),
+        semaphores=(pltpu.SemaphoreType.DMA((BASES,)),),
+    )
 
 
 def on_device(sky_image, dual_coeffs, thresholds):
     basis = lax.axis_index("basis")
     matrices = [lax.dynamic_index_in_dim(jnp.asarray(m), basis, 0, False) for m in operators()]
+    with jax.named_scope("rim_of_arguments"):
+        arguments = shifted(rim_of_arguments(dual_coeffs, thresholds), 1)
     with jax.named_scope("gather_columns"):
         field = lax.all_to_all(jnp.broadcast_to(sky_image, (BASES, ROWS, 128)), "basis", 0, 0)
         field, *matrices = lax.optimization_barrier((field, *matrices))
-    dual_next, whole = local_update(field, dual_coeffs, thresholds, matrices, shifted)
+    dual_next, whole = local_update(field, arguments, dual_coeffs, thresholds, matrices, shifted)
     with jax.named_scope("sum_over_bases"):
         adjoint_image = jnp.sum(lax.all_to_all(whole, "basis", 0, 0), axis=0)
     return (dual_next, adjoint_image)

time: 50.3 us -> 47.6 us (0.946)
  the two profiles are of different devices: /device:TPU:2 before, /device:TPU:105 now
where the time goes in v2:
time: 47.6 us; the launch traced here: 47.1 us
  starting transfers between devices  15 us (32%)
  blocking collectives  11.5 us (24%)
  local copies, waits for them, and re-layouts  6.98 us (15%)
  Pallas kernels  6.3 us (13%)
  waiting for transfers between devices  6.03 us (13%)
  between operations  0.7 us (1%)
  other arithmetic  0.66 us (1%)
    all_to_all x1, blocking collectives, on_device(): adjoint_image = jnp.sum(lax.all_to_all(whole, 'basis', 0, 0), axis=0)  11.5 us
    ppermute x3, starting transfers between devices, shifted(): return lax.ppermute(value, 'strip', pairs)  9.28 us
    pallas_call x8, Pallas kernels, call(): pl.pallas_call(kernel, in_specs=[vmem] * len(operands), out_specs=out_spe...  6.3 us
    ppermute x3, waiting for transfers between devices, shifted(): return lax.ppermute(value, 'strip', pairs)  5.9 us
    all_to_all x1, starting transfers between devices, on_device(): lax.all_to_all(jnp.broadcast_to(sky_image, (BASES, ROWS, 128)), 'basis',...  5.75 us
    squeeze x3, local copies, waits for them, and re-layouts, on_device(): lax.dynamic_index_in_dim(jnp.asarray(m), basis, 0, False)  3.22 us
    unnamed x8, local copies, waits for them, and re-layouts  2.09 us
    broadcast_in_dim x1, local copies, waits for them, and re-layouts, on_device(): jnp.broadcast_to(sky_image, (BASES, ROWS, 128))  1.67 us
  transfers between devices with their start and end apart: 4, of which 2 were waited for; matrix products, arithmetic and copies ran while one was open for 7% of the time, Pallas kernels for 10%

profile of v2, /device:TPU:105, one launch (start us, length us, event | category | flops | bytes accessed | tf_op | source)
XLA Modules:
  0.0 47.1 jit_solution(12661198037127693699)
XLA Ops:
  0.6 1.7 %broadcast_in_dim.3 = f32[8,128,128]{2,1,0:T(8,128)} broadcast(f32[128,128]{1,0:T(8,128)} %param.7), dimensions={1,2} | broadcast | bytes 589824 | tf_op jit(solution)/shard_map/gather_columns/broadcast_in_dim | solution.py:463
  2.3 5.8 %all-to-all-start = ((f32[8,128,128]{2,1,0:T(8,128)}), f32[8,128,128]{2,1,0:T(8,128)S(1)}, u32[]{:S(2)}, u32[]{:S(2)}) async-start(f32[8,128,128]{2,1,0:T(8,128)} %broadcast_in_dim.3), calls=%async_computation | async-start | bytes 1048576 | tf_op jit(solution)/shard_map/gather_columns/all_to_all | solution.py:463
  8.0 0.0 copy-start
  8.1 1.0 %copy-done = f32[1,128,1024]{2,1,0:T(8,128)S(1)} copy-done((f32[1,128,1024]{2,1,0:T(8,128)S(1)}, f32[1,128,1024]{2,1,0:T(8,128)}, u32[]{:S(2)}) %copy-start) | copy-done | bytes 524312
  9.1 0.0 copy-start.2
  9.1 1.0 %copy-done.2 = f32[1,128,1024]{2,1,0:T(8,128)S(1)} copy-done((f32[1,128,1024]{2,1,0:T(8,128)S(1)}, f32[1,128,1024]{2,1,0:T(8,128)}, u32[]{:S(2)}) %copy-start.2) | copy-done | bytes 524312
  10.1 0.0 copy-start.1
  10.1 0.0 copy-start.3
  10.1 0.8 %rim_of_arguments.1 = f32[8,64,128]{2,1,0:T(8,128)} custom-call(f32[1,128,1024]{2,1,0:T(8,128)S(1)} %copy-done, f32[1,128,1024]{2,1,0:T(8,128)S(1)} %copy-done.2), custom_call_target="tpu_custom_call" | custom-call | tf_op jit(solution)/shard_map/rim_of_arguments/rim_of_arguments/pallas_call | solution.py:399
  11.0 4.5 %collective-permute-start.1 = (f32[8,64,128]{2,1,0:T(8,128)}, f32[8,64,128]{2,1,0:T(8,128)S(1)}, u32[]{:S(2)}, u32[]{:S(2)}) collective-permute-start(f32[8,64,128]{2,1,0:T(8,128)} %rim_of_arguments.1), channel_id=1, source_target_pairs={{0,8},{8,16},{16,24},{24,32},{32,40},{40,48},{48,56},{56,64},{64,7... | collective-permute-start | bytes 786440 | tf_op jit(solution)/shard_map/rim_of_arguments/ppermute | solution.py:413
  15.4 1.0 %dynamic-slice_bitcast_fusion.3.rows_ref = bf16[2,384,256]{2,1,0:T(8,128)(2,1)S(1)} fusion(bf16[8,2,384,256]{3,2,1,0:T(8,128)(2,1)} %constant.30.clone, s32[]{:T(128)S(6)} %select_n.9), kind=kLoop, calls=%fused_computation.3 | loop fusion | bytes 786436 | tf_op jit(solution)/shard_map/jit(dynamic_index_in_dim)/squeeze | solution.py:459
  16.5 1.0 %dynamic-slice_bitcast_fusion.rows_back_ref.refs_3_ = bf16[2,128,672]{2,1,0:T(8,128)(2,1)S(1)} fusion(bf16[8,2,128,672]{3,2,1,0:T(8,128)(2,1)} %constant.33.clone, s32[]{:T(128)S(6)} %select_n.9), kind=kLoop, calls=%fused_computation | loop fusion | bytes 688132 | tf_op jit(solution)/shard_map/jit(dynamic_index_in_dim)/squeeze | solution.py:459
  17.5 1.2 %dynamic-slice_bitcast_fusion.1 = (bf16[3,256,256]{2,1,0:T(8,128)(2,1)S(1)}, bf16[3,256,256]{2,1,0:T(8,128)(2,1)S(1)}) fusion(bf16[8,3,256,256]{3,2,1,0:T(8,128)(2,1)} %constant.32.clone, s32[]{:T(128)S(6)} %select_n.9, bf16[8,3,256,256]{3,2,1,0:T(8,128)(2,1)} %constant.31.clone), kind=kLoop, calls=%fused_computation.1 | loop fusion | bytes 1572868 | tf_op jit(solution)/shard_map/jit(dynamic_index_in_dim)/squeeze | solution.py:459
  18.7 0.1 all-to-all-done.image_ref
  18.8 0.6 %rim_coefficients.1 = f32[8,32,128]{2,1,0:T(8,128)S(1)} custom-call(f32[8,128,128]{2,1,0:T(8,128)S(1)} %all-to-all-done.image_ref, bf16[2,384,256]{2,1,0:T(8,128)(2,1)S(1)} %dynamic-slice_bitcast_fusion.3.rows_ref, bf16[3,256,256]{2,1,0:T(8,128)(2,1)S(1)} %get-tuple-element.15.columns_ref), custom_call_target="tpu_custom_call" | custom-call | tf_op jit(solution)/shard_map/rim_coefficients/pallas_call | solution.py:399
  19.4 4.7 %collective-permute-start = (f32[8,32,128]{2,1,0:T(8,128)S(1)}, f32[8,32,128]{2,1,0:T(8,128)S(1)}, u32[]{:S(2)}, u32[]{:S(2)}) collective-permute-start(f32[8,32,128]{2,1,0:T(8,128)S(1)} %rim_coefficients.1), channel_id=1, source_target_pairs={{0,8},{8,16},{16,24},{24,32},{32,40},{40,48},{48,56},{56,64},{64,7... | collective-permute-start | bytes 393224 | tf_op jit(solution)/shard_map/rim_coefficients/ppermute | solution.py:413
  24.1 0.0 copy-done.1
  24.1 0.0 copy-done.3
  24.1 1.1 %own_update.1.fresh_ref = f32[8,128,128]{2,1,0:T(8,128)S(1)} custom-call(f32[8,128,128]{2,1,0:T(8,128)S(1)} %all-to-all-done.image_ref, bf16[2,384,256]{2,1,0:T(8,128)(2,1)S(1)} %dynamic-slice_bitcast_fusion.3.rows_ref, bf16[3,256,256]{2,1,0:T(8,128)(2,1)S(1)} %get-tuple-element.15.columns_ref, f32[1,128,1024]{2,1,0:T(8,128)S(1)} %copy-done.1, ...), custom_call_target="tpu_custom_call" | custom-call | tf_op jit(solution)/shard_map/own_update/pallas_call | solution.py:399
  25.2 1.3 %own_rows.1.refs_0_ = f32[8,128,128]{2,1,0:T(8,128)S(1)} custom-call(f32[8,128,128]{2,1,0:T(8,128)S(1)} %own_update.1.fresh_ref, bf16[3,256,256]{2,1,0:T(8,128)(2,1)S(1)} %get-tuple-element.16.back_ref.refs_2_, bf16[2,128,672]{2,1,0:T(8,128)(2,1)S(1)} %dynamic-slice_bitcast_fusion.rows_back_ref.refs_3_), custom_call_target="tpu_custom_call" | custom-call | tf_op jit(solution)/shard_map/own_rows/pallas_call | solution.py:399
  26.4 0.0 collective-permute-done.1.arguments_ref
  26.5 0.6 %previous_rim.1.before_ref = f32[8,64,128]{2,1,0:T(8,128)S(1)} custom-call(f32[8,128,128]{2,1,0:T(8,128)S(1)} %all-to-all-done.image_ref, bf16[2,384,256]{2,1,0:T(8,128)(2,1)S(1)} %dynamic-slice_bitcast_fusion.3.rows_ref, bf16[3,256,256]{2,1,0:T(8,128)(2,1)S(1)} %get-tuple-element.15.columns_ref, f32[8,64,128]{2,1,0:T(8,128)S(1)} %collective-permute-done.1.arguments_ref), custom_call_target="tpu_custom_call" | custom-call | tf_op jit(solution)/shard_map/previous_rim/pallas_call | solution.py:399
  27.1 0.0 collective-permute-done.rim_ref
  27.1 0.1 collective-permute-start.2
  27.2 0.6 %previous_rows.1.own_ref = f32[8,128,128]{2,1,0:T(8,128)S(1)} custom-call(f32[8,128,128]{2,1,0:T(8,128)S(1)} %own_rows.1.refs_0_, f32[8,32,128]{2,1,0:T(8,128)S(1)} %rim_update.1.refs_1_, bf16[3,256,256]{2,1,0:T(8,128)(2,1)S(1)} %get-tuple-element.16.back_ref.refs_2_, bf16[2,128,672]{2,1,0:T(8,128)(2,1)S(1)} %dynamic-slice_bitcast_fusion.rows_back_ref.refs_3_), custom_call_target="tpu_custom_call" | custom-call | tf_op jit(solution)/shard_map/previous_rows/pallas_call | solution.py:399
  27.8 5.9 %collective-permute-done.2.rim_ref = f32[8,32,128]{2,1,0:T(8,128)S(1)} collective-permute-done((f32[8,32,128]{2,1,0:T(8,128)S(1)}, f32[8,32,128]{2,1,0:T(8,128)S(1)}, u32[]{:S(2)}, u32[]{:S(2)}) %collective-permute-start.2) | collective-permute-done | bytes 131104 | tf_op jit(solution)/shard_map/rim_of_update/ppermute | solution.py:413
  33.7 1.3 %finish.1 = (f32[1,128,1024]{2,1,0:T(8,128)}, f32[8,128,128]{2,1,0:T(8,128)S(1)}) custom-call(f32[8,128,128]{2,1,0:T(8,128)S(1)} %previous_rows.1.own_ref, f32[8,32,128]{2,1,0:T(8,128)S(1)} %collective-permute-done.2.rim_ref, f32[8,128,128]{2,1,0:T(8,128)S(1)} %own_update.1.fresh_ref, bf16[3,256,256]{2,1,0:T(8,128)(2,1)S(1)} %get-tuple-element.16.back_ref.refs_2_, ...), custom_call_target="tpu_custom_call" | custom-call | tf_op jit(solution)/shard_map/finish/pallas_call | solution.py:399
  35.0 11.5 %all_to_all.10 = f32[8,128,128]{2,1,0:T(8,128)S(1)} all-to-all(f32[8,128,128]{2,1,0:T(8,128)S(1)} %get-tuple-element.23), channel_id=1, replica_groups=mesh['strip'=32,'basis'=8] {'basis'}, dimensions={0} | all-to-all | bytes 1048576 | tf_op jit(solution)/shard_map/sum_over_bases/all_to_all | solution.py:467
  46.5 0.7 %reduce_sum.9 = f32[128,128]{1,0:T(8,128)} reduce(f32[8,128,128]{2,1,0:T(8,128)S(1)} %all_to_all.10, f32[]{:T(128)} %constant.29.clone.1), dimensions={0}, to_apply=%region_0.1 | reduce | flops 114688 | bytes 589828 | tf_op jit(solution)/shard_map/sum_over_bases/reduce_sum | solution.py:467
  (1 shorter events, 0.0 us)
Async XLA Ops:
  2.3 16.5 %all-to-all-start = ((f32[8,128,128]{2,1,0:T(8,128)}), f32[8,128,128]{2,1,0:T(8,128)S(1)}, u32[]{:S(2)}, u32[]{:S(2)}) async-start(f32[8,128,128]{2,1,0:T(8,128)} %broadcast_in_dim.3), calls=%async_computation | async-start | bytes 1048576 | tf_op jit(solution)/shard_map/gather_columns/all_to_all | solution.py:463
  8.0 1.0 %copy-start = (f32[1,128,1024]{2,1,0:T(8,128)S(1)}, f32[1,128,1024]{2,1,0:T(8,128)}, u32[]{:S(2)}) copy-start(f32[1,128,1024]{2,1,0:T(8,128)} %dual_ref.3) | copy-start | bytes 1572868
  9.1 1.0 %copy-start.2 = (f32[1,128,1024]{2,1,0:T(8,128)S(1)}, f32[1,128,1024]{2,1,0:T(8,128)}, u32[]{:S(2)}) copy-start(f32[1,128,1024]{2,1,0:T(8,128)} %limit_ref.3) | copy-start | bytes 1572868
  10.1 14.0 %copy-start.1 = (f32[1,128,1024]{2,1,0:T(8,128)S(1)}, f32[1,128,1024]{2,1,0:T(8,128)}, u32[]{:S(2)}) copy-start(f32[1,128,1024]{2,1,0:T(8,128)} %dual_ref.3) | copy-start | bytes 1572868
  10.1 14.0 %copy-start.3 = (f32[1,128,1024]{2,1,0:T(8,128)S(1)}, f32[1,128,1024]{2,1,0:T(8,128)}, u32[]{:S(2)}) copy-start(f32[1,128,1024]{2,1,0:T(8,128)} %limit_ref.3) | copy-start | bytes 1572868
  11.0 15.5 %collective-permute-start.1 = (f32[8,64,128]{2,1,0:T(8,128)}, f32[8,64,128]{2,1,0:T(8,128)S(1)}, u32[]{:S(2)}, u32[]{:S(2)}) collective-permute-start(f32[8,64,128]{2,1,0:T(8,128)} %rim_of_arguments.1), channel_id=1, source_target_pairs={{0,8},{8,16},{16,24},{24,32},{32,40},{40,48},{48,56},{56,64},{64,7... | collective-permute-start | bytes 786440 | tf_op jit(solution)/shard_map/rim_of_arguments/ppermute | solution.py:413
  19.4 7.7 %collective-permute-start = (f32[8,32,128]{2,1,0:T(8,128)S(1)}, f32[8,32,128]{2,1,0:T(8,128)S(1)}, u32[]{:S(2)}, u32[]{:S(2)}) collective-permute-start(f32[8,32,128]{2,1,0:T(8,128)S(1)} %rim_coefficients.1), channel_id=1, source_target_pairs={{0,8},{8,16},{16,24},{24,32},{32,40},{40,48},{48,56},{56,64},{64,7... | collective-permute-start | bytes 393224 | tf_op jit(solution)/shard_map/rim_coefficients/ppermute | solution.py:413
  27.1 6.6 %collective-permute-start.2 = (f32[8,32,128]{2,1,0:T(8,128)S(1)}, f32[8,32,128]{2,1,0:T(8,128)S(1)}, u32[]{:S(2)}, u32[]{:S(2)}) collective-permute-start(f32[8,32,128]{2,1,0:T(8,128)S(1)} %rim_update.1.refs_1_), channel_id=1, source_target_pairs={{0,248},{8,0},{16,8},{24,16},{32,24},{40,32},{48,40},{56,48},{64,5... | collective-permute-start | bytes 393224 | tf_op jit(solution)/shard_map/rim_of_update/ppermute | solution.py:413

commit v3 on v2

--- a/solution.py
+++ b/solution.py
@@ -174,11 +174,11 @@
     rim = np.stack([m[:, :ROWS] for m in rims])
     columns = np.stack([column_operators(levels) for levels in filters])
     columns_back = np.concatenate([columns[:, :, 128:].transpose(0, 1, 3, 2), columns[:, :, :128].transpose(0, 1, 3, 2)], axis=2)
-    rows = np.concatenate([before, own, rim], axis=1)
-    gap = np.zeros((BASES, ROWS, 96))
-    own_back, before_back, rim_back = (m.transpose(0, 2, 1) for m in (own, before, rim))
+    levels = (slice(0, 16), slice(16, 48), slice(48, 80))
+    both = np.concatenate([m[:, at] for at in levels for m in (before, rim)], axis=1)
+    rows = np.concatenate([own, both], axis=1)
     rows_back = np.concatenate(
-        [own_back, gap[:, :, :32], before_back, before_back, gap, rim_back, rim_back], axis=2
+        [own.transpose(0, 2, 1), np.zeros((BASES, ROWS, 32)), both.transpose(0, 2, 1)], axis=2
     )
     return [
         np.stack(two_parts(np.concatenate([rows, rows], axis=2)), axis=1),
@@ -217,7 +217,7 @@
 
 
 OWN_SPANS = ((0, 128), (128, 192), (192, 224))
-RIM_SPANS = ((0, 16), (16, 48), (48, 80))
+RIM_SPANS = ((0, 32), (32, 96), (96, 160))
 
 
 def lane_masks(rows):
@@ -262,19 +262,21 @@
             send_ref[b, 32 * i : 32 * i + 32] = packed_rim(field, even)
 
 
-def rim_coefficients_kernel(first, image_ref, rows_ref, columns_ref, send_ref, high, low):
-    row_product(image_ref, rows_ref, slice(first, first + 80), high, low)
+def rim_coefficients_kernel(image_ref, rows_ref, columns_ref, before_ref, rim_ref, high, low):
+    row_product(image_ref, rows_ref, slice(BANDS, BANDS + 160), high, low)
     even, fourth, third = lane_masks(8)
-    for b, (one, two, three) in enumerate(column_product((high, low), RIM_SPANS, columns_ref)):
-        send = send_ref.at[b]
-        send[0:8] = one[0:8]
-        send[8:16] = jnp.where(even, jnp.where(third, three[24:32], two[16:24]), one[8:16])
-        send[16:24] = pack(jnp.where(fourth, three[16:24], two[0:8]), two[8:16], even)
-        send[24:32] = pack(three[0:8], three[8:16], even)
+    for b, levels in enumerate(column_product((high, low), RIM_SPANS, columns_ref)):
+        for i, ref in enumerate((before_ref, rim_ref)):
+            one, two, three = (part[i * part.shape[0] // 2 : (i + 1) * part.shape[0] // 2] for part in levels)
+            send = ref.at[b]
+            send[0:8] = one[0:8]
+            send[8:16] = jnp.where(even, jnp.where(third, three[24:32], two[16:24]), one[8:16])
+            send[16:24] = pack(jnp.where(fourth, three[16:24], two[0:8]), two[8:16], even)
+            send[24:32] = pack(three[0:8], three[8:16], even)
 
 
 def own_update_kernel(image_ref, rows_ref, columns_ref, dual_ref, limit_ref, fresh_ref, high, low):
-    row_product(image_ref, rows_ref, slice(80, 304), high, low)
+    row_product(image_ref, rows_ref, slice(0, BANDS), high, low)
     even, _, _ = lane_masks(64)
     _, fourth, _ = lane_masks(32)
     for b, (one, two, three) in enumerate(column_product((high, low), OWN_SPANS, columns_ref)):
@@ -290,15 +292,16 @@
             field[pl.ds(start, 8, 4), :] = jnp.where(mask[:8], 0.0, field[pl.ds(start, 8, 4), :])
 
 
-def previous_rim_kernel(image_ref, rows_ref, columns_ref, arguments_ref, out_ref, high, low, partial):
-    rim_coefficients_kernel(0, image_ref, rows_ref, columns_ref, partial, high, low)
-    out_ref[:, :32] = partial[...] + arguments_ref[:, :32]
-    out_ref[:, 32:] = arguments_ref[:, 32:]
-
-
-def rim_update_kernel(rim_ref, before_ref, send_ref):
-    limit = before_ref[:, 32:]
-    send_ref[...] = jnp.minimum(jnp.maximum(before_ref[:, :32] + rim_ref[...], -limit), limit)
+def add_rows_back(tiles, rows_back_ref, lanes, out_ref, own_ref=None):
+    row_op = jnp.concatenate([rows_back_ref[0, :, lanes], rows_back_ref[1, :, lanes]], axis=0)
+    tiles = [jnp.concatenate(bands, axis=0) for bands in tiles]
+    for t in range(TILES):
+        first, second = split(join(tiles, t))
+        part = dot(row_op, first)
+        part = part[:ROWS] + (part[ROWS:] + dot(row_op[:ROWS], second))
+        for h in range(2):
+            half = part[:, 128 * h : 128 * h + 128]
+            out_ref[2 * t + h] = half if own_ref is None else own_ref[2 * t + h] + half
 
 
 def own_rows_kernel(fresh_ref, back_ref, rows_back_ref, out_ref, high, low):
@@ -315,58 +318,34 @@
             ref[:, 128 * b + 128 : 128 * b + 256] = part
             if b == 7:
                 ref[:, 0:128] = part
-    row_op = jnp.concatenate([rows_back_ref[0, :, :BANDS], rows_back_ref[1, :, :BANDS]], axis=0)
-    tiles = [jnp.concatenate(bands, axis=0) for bands in column_product((high, low), OWN_SPANS, back_ref)]
-    for t in range(TILES):
-        first, second = split(join(tiles, t))
-        part = dot(row_op, first)
-        part = part[:ROWS] + (part[ROWS:] + dot(row_op[:ROWS], second))
-        out_ref[2 * t] = part[:, :128]
-        out_ref[2 * t + 1] = part[:, 128:]
-
-
-def add_rim_rows(first, own_ref, rim_ref, back_ref, rows_back_ref, out_ref, high, low):
+    add_rows_back(column_product((high, low), OWN_SPANS, back_ref), rows_back_ref, slice(0, BANDS), out_ref)
+
+
+def rim_update(first, second, arguments):
+    limit = arguments[32:]
+    return jnp.minimum(jnp.maximum(arguments[:32] + (first[...] + second[...]), -limit), limit)
+
+
+def rim_bands_back(rim):
     even, fourth, third = lane_masks(8)
-    for b in range(8):
-        rim = rim_ref.at[b]
-        odd_rows, even_rows, second, coarse = rim[0:8], rim[8:16], rim[16:24], rim[24:32]
-        parts = split(
-            jnp.concatenate(
-                [
-                    odd_rows,
-                    jnp.where(even, 0.0, even_rows),
-                    jnp.where(fourth, 0.0, second),
-                    unpack_second(second),
-                    jnp.where(third, 0.0, even_rows),
-                    jnp.zeros_like(coarse),
-                    coarse,
-                    unpack_second(coarse),
-                    second,
-                    even_rows,
-                ],
-                axis=0,
-            )
-        )
-        for ref, part in zip((high, low), parts):
-            ref[:, 128 * b + 128 : 128 * b + 256] = part
-            if b == 7:
-                ref[:, 0:128] = part
-    tiles = [jnp.concatenate(bands, axis=0) for bands in column_product((high, low), RIM_SPANS, back_ref)]
-    for t in range(TILES):
-        part = twice_product(rows_back_ref, (slice(None), slice(first, first + 160)), join(tiles, t))
-        out_ref[2 * t] = own_ref[2 * t] + part[:, :128]
-        out_ref[2 * t + 1] = own_ref[2 * t + 1] + part[:, 128:]
-
-
-def rows_of_previous_kernel(*refs):
-    add_rim_rows(256, *refs)
-
-
-def finish_kernel(own_ref, rim_ref, fresh_ref, back_ref, rows_back_ref, next_ref, out_ref, high, low, fields, sent):
+    odd_rows, even_rows, second, coarse = rim[0:8], rim[8:16], rim[16:24], rim[24:32]
+    return (
+        [odd_rows, jnp.where(even, 0.0, even_rows)],
+        [jnp.where(fourth, 0.0, second), unpack_second(second), jnp.where(third, 0.0, even_rows), jnp.zeros_like(coarse)],
+        [coarse, unpack_second(coarse), second, even_rows],
+    )
+
+
+def finish_kernel(
+    own_ref, fresh_ref, rim_ref, ahead_ref, arguments_ref, before_ref, behind_ref, previous_ref, back_ref, rows_back_ref,
+    next_ref, out_ref, high, low, fields, sent,
+):
     even, fourth, _ = lane_masks(8)
     copies = []
     for b in range(8):
-        field, rim = fields.at[b], rim_ref.at[b]
+        field = fields.at[b]
+        rim = rim_update(rim_ref.at[b], ahead_ref.at[b], arguments_ref[b])
+        previous = rim_update(before_ref.at[b], behind_ref.at[b], previous_ref[b])
         field[...] = fresh_ref[b]
         second, third = rim[16:24], rim[24:32]
         field[pl.ds(113, 8, 2), :] = rim[0:8]
@@ -380,7 +359,13 @@
             field[pl.ds(start, 8, 4), :] = jnp.where(mask, value, field[pl.ds(start, 8, 4), :])
         copies.append(pltpu.make_async_copy(field, next_ref.at[0, :, pl.ds(128 * b, 128)], sent.at[b]))
         copies[b].start()
-    add_rim_rows(512, own_ref, rim_ref, back_ref, rows_back_ref, out_ref, high, low)
+        levels = zip(rim_bands_back(previous), rim_bands_back(rim))
+        parts = split(jnp.concatenate([rows for first, second in levels for rows in first + second], axis=0))
+        for ref, part in zip((high, low), parts):
+            ref[:, 128 * b + 128 : 128 * b + 256] = part
+            if b == 7:
+                ref[:, 0:128] = part
+    add_rows_back(column_product((high, low), RIM_SPANS, back_ref), rows_back_ref, slice(256, 416), out_ref, own_ref)
     for copy in copies:
         copy.wait()
 
@@ -391,7 +376,7 @@
 RIMS = ((BASES, 64, 128), F32)
 WOVEN = ((1, ROWS, COLS), F32)
 WIDE = ((BANDS, COLS + 128), BF16)
-RIM_WIDE = ((80, COLS + 128), BF16)
+RIM_WIDE = ((160, COLS + 128), BF16)
 
 
 def call(kernel, name, out_shape, *operands, scratch=(), out_specs=None, semaphores=()):
@@ -421,33 +406,23 @@
     return packed
 
 
-def local_update(field, arguments, dual_coeffs, thresholds, matrices, shift):
+def local_update(field, arguments, previous, dual_coeffs, thresholds, matrices, shift):
     rows, columns, columns_back, rows_back = matrices
-    (rim,) = call(
-        functools.partial(rim_coefficients_kernel, 304), "rim_coefficients", (RIM,), field, rows, columns,
-        scratch=(RIM_WIDE, RIM_WIDE),
+    before, rim = call(
+        rim_coefficients_kernel, "rim_coefficients", (RIM, RIM), field, rows, columns, scratch=(RIM_WIDE, RIM_WIDE)
     )
     with jax.named_scope("rim_coefficients"):
-        rim = shift(rim, 1)
+        behind = shift(rim, 1)
+        ahead = shift(before, -1)
     (fresh,) = call(
         own_update_kernel, "own_update", (FIELD,), field, rows, columns, dual_coeffs, thresholds, scratch=(WIDE, WIDE)
     )
     (own,) = call(own_rows_kernel, "own_rows", (FIELD,), fresh, columns_back, rows_back, scratch=(WIDE, WIDE))
-    (before,) = call(
-        previous_rim_kernel, "previous_rim", (RIMS,), field, rows, columns, arguments, scratch=(RIM_WIDE, RIM_WIDE, RIM)
-    )
-    rim, before, fresh, own = lax.optimization_barrier((rim, before, fresh, own))
-    (update,) = call(rim_update_kernel, "rim_update", (RIM,), rim, before)
-    with jax.named_scope("rim_of_update"):
-        rim = shift(update, -1)
-    (own,) = call(
-        rows_of_previous_kernel, "previous_rows", (FIELD,), own, update, columns_back, rows_back, scratch=(RIM_WIDE, RIM_WIDE)
-    )
     return call(
         finish_kernel,
         "finish",
         (WOVEN, FIELD),
-        own, rim, fresh, columns_back, rows_back,
+        own, fresh, rim, ahead, arguments, before, behind, previous, columns_back, rows_back,
         scratch=(RIM_WIDE, RIM_WIDE, FIELD),
         out_specs=(pl.BlockSpec(memory_space=pl.ANY), pl.BlockSpec(memory_space=pltpu.VMEM)),
         semaphores=(pltpu.SemaphoreType.DMA((BASES,)),),
@@ -458,11 +433,12 @@
     basis = lax.axis_index("basis")
     matrices = [lax.dynamic_index_in_dim(jnp.asarray(m), basis, 0, False) for m in operators()]
     with jax.named_scope("rim_of_arguments"):
-        arguments = shifted(rim_of_arguments(dual_coeffs, thresholds), 1)
+        arguments = rim_of_arguments(dual_coeffs, thresholds)
+        previous = shifted(arguments, 1)
     with jax.named_scope("gather_columns"):
         field = lax.all_to_all(jnp.broadcast_to(sky_image, (BASES, ROWS, 128)), "basis", 0, 0)
         field, *matrices = lax.optimization_barrier((field, *matrices))
-    dual_next, whole = local_update(field, arguments, dual_coeffs, thresholds, matrices, shifted)
+    dual_next, whole = local_update(field, arguments, previous, dual_coeffs, thresholds, matrices, shifted)
     with jax.named_scope("sum_over_bases"):
         adjoint_image = jnp.sum(lax.all_to_all(whole, "basis", 0, 0), axis=0)
     return (dual_next, adjoint_image)

time: 47.6 us -> 46.2 us (0.971)
  the two profiles are of different devices: /device:TPU:105 before, /device:TPU:2 now
where the time goes in v3:
time: 46.2 us; the launch traced here: 45.8 us
  blocking collectives  16.5 us (36%)
  starting transfers between devices  11.6 us (25%)
  local copies, waits for them, and re-layouts  6.93 us (15%)
  waiting for transfers between devices  5.03 us (11%)
  Pallas kernels  4.35 us (9%)
  between operations  0.69 us (1%)
  other arithmetic  0.66 us (1%)
    all_to_all x1, blocking collectives, on_device(): adjoint_image = jnp.sum(lax.all_to_all(whole, 'basis', 0, 0), axis=0)  16.5 us
    all_to_all x1, starting transfers between devices, on_device(): lax.all_to_all(jnp.broadcast_to(sky_image, (BASES, ROWS, 128)), 'basis',...  7.59 us
    all_to_all x1, waiting for transfers between devices, on_device(): lax.all_to_all(jnp.broadcast_to(sky_image, (BASES, ROWS, 128)), 'basis',...  4.7 us
    pallas_call x5, Pallas kernels, call(): pl.pallas_call(kernel, in_specs=[vmem] * len(operands), out_specs=out_spe...  4.35 us
    ppermute x3, starting transfers between devices, shifted(): return lax.ppermute(value, 'strip', pairs)  4 us
    squeeze x3, local copies, waits for them, and re-layouts, on_device(): lax.dynamic_index_in_dim(jnp.asarray(m), basis, 0, False)  3.18 us
    unnamed x8, local copies, waits for them, and re-layouts  2.09 us
    broadcast_in_dim x1, local copies, waits for them, and re-layouts, on_device(): jnp.broadcast_to(sky_image, (BASES, ROWS, 128))  1.67 us
  transfers between devices with their start and end apart: 4, of which 2 were waited for; matrix products, arithmetic and copies ran while one was open for 7% of the time, Pallas kernels for 7%

profile of v3, /device:TPU:2, one launch (start us, length us, event | category | flops | bytes accessed | tf_op | source)
XLA Modules:
  0.0 45.8 jit_solution(10756683619581346285)
XLA Ops:
  0.6 1.7 %broadcast_in_dim.3 = f32[8,128,128]{2,1,0:T(8,128)} broadcast(f32[128,128]{1,0:T(8,128)} %param.7), dimensions={1,2} | broadcast | bytes 589824 | tf_op jit(solution)/shard_map/gather_columns/broadcast_in_dim | solution.py:439
  2.3 0.0 copy-start.1
  2.3 0.0 copy-start.3
  2.3 7.6 %all-to-all-start = ((f32[8,128,128]{2,1,0:T(8,128)}), f32[8,128,128]{2,1,0:T(8,128)S(1)}, u32[]{:S(2)}, u32[]{:S(2)}) async-start(f32[8,128,128]{2,1,0:T(8,128)} %broadcast_in_dim.3), calls=%async_computation | async-start | bytes 1048576 | tf_op jit(solution)/shard_map/gather_columns/all_to_all | solution.py:439
  9.9 0.0 copy-start
  9.9 1.0 %copy-done = f32[1,128,1024]{2,1,0:T(8,128)S(1)} copy-done((f32[1,128,1024]{2,1,0:T(8,128)S(1)}, f32[1,128,1024]{2,1,0:T(8,128)}, u32[]{:S(2)}) %copy-start) | copy-done | bytes 524312
  10.9 0.0 copy-start.2
  10.9 1.0 %copy-done.2 = f32[1,128,1024]{2,1,0:T(8,128)S(1)} copy-done((f32[1,128,1024]{2,1,0:T(8,128)S(1)}, f32[1,128,1024]{2,1,0:T(8,128)}, u32[]{:S(2)}) %copy-start.2) | copy-done | bytes 524312
  12.0 0.1 rim_of_arguments.1.arguments_ref
  12.1 0.1 collective-permute-start.2
  12.2 1.0 %dynamic-slice_bitcast_fusion.3.rows_back_ref = bf16[2,128,416]{2,1,0:T(8,128)(2,1)S(1)} fusion(bf16[8,2,128,416]{3,2,1,0:T(8,128)(2,1)} %constant.33.clone, s32[]{:T(128)S(6)} %select_n.9), kind=kLoop, calls=%fused_computation.3 | loop fusion | bytes 425988 | tf_op jit(solution)/shard_map/jit(dynamic_index_in_dim)/squeeze | solution.py:434
  13.2 1.0 %dynamic-slice_bitcast_fusion.2.rows_ref = bf16[2,384,256]{2,1,0:T(8,128)(2,1)S(1)} fusion(bf16[8,2,384,256]{3,2,1,0:T(8,128)(2,1)} %constant.30.clone, s32[]{:T(128)S(6)} %select_n.9), kind=kLoop, calls=%fused_computation.2 | loop fusion | bytes 786436 | tf_op jit(solution)/shard_map/jit(dynamic_index_in_dim)/squeeze | solution.py:434
  14.2 1.2 %dynamic-slice_bitcast_fusion = (bf16[3,256,256]{2,1,0:T(8,128)(2,1)S(1)}, bf16[3,256,256]{2,1,0:T(8,128)(2,1)S(1)}) fusion(bf16[8,3,256,256]{3,2,1,0:T(8,128)(2,1)} %constant.32.clone, s32[]{:T(128)S(6)} %select_n.9, bf16[8,3,256,256]{3,2,1,0:T(8,128)(2,1)} %constant.31.clone), kind=kLoop, calls=%fused_computation | loop fusion | bytes 1572868 | tf_op jit(solution)/shard_map/jit(dynamic_index_in_dim)/squeeze | solution.py:434
  15.4 4.7 %all-to-all-done.image_ref = f32[8,128,128]{2,1,0:T(8,128)S(1)} async-done(((f32[8,128,128]{2,1,0:T(8,128)}), f32[8,128,128]{2,1,0:T(8,128)S(1)}, u32[]{:S(2)}, u32[]{:S(2)}) %all-to-all-start) | async-done | bytes 524320 | tf_op jit(solution)/shard_map/gather_columns/all_to_all | solution.py:439
  20.1 0.8 %rim_coefficients.1 = (f32[8,32,128]{2,1,0:T(8,128)S(1)}, f32[8,32,128]{2,1,0:T(8,128)S(1)}) custom-call(f32[8,128,128]{2,1,0:T(8,128)S(1)} %all-to-all-done.image_ref, bf16[2,384,256]{2,1,0:T(8,128)(2,1)S(1)} %dynamic-slice_bitcast_fusion.2.rows_ref, bf16[3,256,256]{2,1,0:T(8,128)(2,1)S(1)} %get-tuple-element.13.columns_ref), custom_call_target="tpu_custom_call" | custom-call | tf_op jit(solution)/shard_map/rim_coefficients/pallas_call | solution.py:384
  20.9 0.1 collective-permute-start.1
  21.0 3.8 %collective-permute-start = (f32[8,32,128]{2,1,0:T(8,128)S(1)}, f32[8,32,128]{2,1,0:T(8,128)S(1)}, u32[]{:S(2)}, u32[]{:S(2)}) collective-permute-start(f32[8,32,128]{2,1,0:T(8,128)S(1)} %get-tuple-element.17.before_ref), channel_id=1, source_target_pairs={{0,248},{8,0},{16,8},{24,16},{32,24},{40,32},{48,40},{56,48},{64,5... | collective-permute-start | bytes 393224 | tf_op jit(solution)/shard_map/rim_coefficients/ppermute | solution.py:398
  24.8 0.0 copy-done.1
  24.8 0.0 copy-done.3
  24.9 1.0 %own_update.1.fresh_ref = f32[8,128,128]{2,1,0:T(8,128)S(1)} custom-call(f32[8,128,128]{2,1,0:T(8,128)S(1)} %all-to-all-done.image_ref, bf16[2,384,256]{2,1,0:T(8,128)(2,1)S(1)} %dynamic-slice_bitcast_fusion.2.rows_ref, bf16[3,256,256]{2,1,0:T(8,128)(2,1)S(1)} %get-tuple-element.13.columns_ref, f32[1,128,1024]{2,1,0:T(8,128)S(1)} %copy-done.1, ...), custom_call_target="tpu_custom_call" | custom-call | tf_op jit(solution)/shard_map/own_update/pallas_call | solution.py:384
  25.9 1.3 %own_rows.1.own_ref = f32[8,128,128]{2,1,0:T(8,128)S(1)} custom-call(f32[8,128,128]{2,1,0:T(8,128)S(1)} %own_update.1.fresh_ref, bf16[3,256,256]{2,1,0:T(8,128)(2,1)S(1)} %get-tuple-element.14.back_ref, bf16[2,128,416]{2,1,0:T(8,128)(2,1)S(1)} %dynamic-slice_bitcast_fusion.3.rows_back_ref), custom_call_target="tpu_custom_call" | custom-call | tf_op jit(solution)/shard_map/own_rows/pallas_call | solution.py:384
  27.2 0.0 collective-permute-done.2.previous_ref
  27.2 0.3 collective-permute-done.1.behind_ref
  27.5 0.0 collective-permute-done.ahead_ref
  27.5 1.1 %finish.1 = (f32[1,128,1024]{2,1,0:T(8,128)}, f32[8,128,128]{2,1,0:T(8,128)S(1)}) custom-call(f32[8,128,128]{2,1,0:T(8,128)S(1)} %own_rows.1.own_ref, f32[8,128,128]{2,1,0:T(8,128)S(1)} %own_update.1.fresh_ref, f32[8,32,128]{2,1,0:T(8,128)S(1)} %get-tuple-element.16.rim_ref, f32[8,32,128]{2,1,0:T(8,128)S(1)} %collective-permute-done.ahead_ref, ...), custom_call_target="tpu_custom_call" | custom-call | tf_op jit(solution)/shard_map/finish/pallas_call | solution.py:384
  28.6 16.5 %all_to_all.10 = f32[8,128,128]{2,1,0:T(8,128)S(1)} all-to-all(f32[8,128,128]{2,1,0:T(8,128)S(1)} %get-tuple-element.19), channel_id=1, replica_groups=mesh['strip'=32,'basis'=8] {'basis'}, dimensions={0} | all-to-all | bytes 1048576 | tf_op jit(solution)/shard_map/sum_over_bases/all_to_all | solution.py:443
  45.1 0.7 %reduce_sum.9 = f32[128,128]{1,0:T(8,128)} reduce(f32[8,128,128]{2,1,0:T(8,128)S(1)} %all_to_all.10, f32[]{:T(128)} %constant.29.clone.1), dimensions={0}, to_apply=%region_0.1 | reduce | flops 114688 | bytes 589828 | tf_op jit(solution)/shard_map/sum_over_bases/reduce_sum | solution.py:443
Async XLA Ops:
  2.3 22.6 %copy-start.1 = (f32[1,128,1024]{2,1,0:T(8,128)S(1)}, f32[1,128,1024]{2,1,0:T(8,128)}, u32[]{:S(2)}) copy-start(f32[1,128,1024]{2,1,0:T(8,128)} %dual_ref.3) | copy-start | bytes 1572868
  2.3 22.6 %copy-start.3 = (f32[1,128,1024]{2,1,0:T(8,128)S(1)}, f32[1,128,1024]{2,1,0:T(8,128)}, u32[]{:S(2)}) copy-start(f32[1,128,1024]{2,1,0:T(8,128)} %limit_ref.3) | copy-start | bytes 1572868
  2.3 17.8 %all-to-all-start = ((f32[8,128,128]{2,1,0:T(8,128)}), f32[8,128,128]{2,1,0:T(8,128)S(1)}, u32[]{:S(2)}, u32[]{:S(2)}) async-start(f32[8,128,128]{2,1,0:T(8,128)} %broadcast_in_dim.3), calls=%async_computation | async-start | bytes 1048576 | tf_op jit(solution)/shard_map/gather_columns/all_to_all | solution.py:439
  9.9 1.0 %copy-start = (f32[1,128,1024]{2,1,0:T(8,128)S(1)}, f32[1,128,1024]{2,1,0:T(8,128)}, u32[]{:S(2)}) copy-start(f32[1,128,1024]{2,1,0:T(8,128)} %dual_ref.3) | copy-start | bytes 1572868
  10.9 1.0 %copy-start.2 = (f32[1,128,1024]{2,1,0:T(8,128)S(1)}, f32[1,128,1024]{2,1,0:T(8,128)}, u32[]{:S(2)}) copy-start(f32[1,128,1024]{2,1,0:T(8,128)} %limit_ref.3) | copy-start | bytes 1572868
  12.1 15.1 %collective-permute-start.2 = (f32[8,64,128]{2,1,0:T(8,128)S(1)}, f32[8,64,128]{2,1,0:T(8,128)S(1)}, u32[]{:S(2)}, u32[]{:S(2)}) collective-permute-start(f32[8,64,128]{2,1,0:T(8,128)S(1)} %rim_of_arguments.1.arguments_ref), channel_id=1, source_target_pairs={{0,8},{8,16},{16,24},{24,32},{32,40},{40,48},{48,56},{56,64},{64,7... | collective-permute-start | bytes 786440 | tf_op jit(solution)/shard_map/rim_of_arguments/ppermute | solution.py:398
  20.9 6.6 %collective-permute-start.1 = (f32[8,32,128]{2,1,0:T(8,128)S(1)}, f32[8,32,128]{2,1,0:T(8,128)S(1)}, u32[]{:S(2)}, u32[]{:S(2)}) collective-permute-start(f32[8,32,128]{2,1,0:T(8,128)S(1)} %get-tuple-element.16.rim_ref), channel_id=1, source_target_pairs={{0,8},{8,16},{16,24},{24,32},{32,40},{40,48},{48,56},{56,64},{64,7... | collective-permute-start | bytes 393224 | tf_op jit(solution)/shard_map/rim_coefficients/ppermute | solution.py:398
  21.0 6.5 %collective-permute-start = (f32[8,32,128]{2,1,0:T(8,128)S(1)}, f32[8,32,128]{2,1,0:T(8,128)S(1)}, u32[]{:S(2)}, u32[]{:S(2)}) collective-permute-start(f32[8,32,128]{2,1,0:T(8,128)S(1)} %get-tuple-element.17.before_ref), channel_id=1, source_target_pairs={{0,248},{8,0},{16,8},{24,16},{32,24},{40,32},{48,40},{56,48},{64,5... | collective-permute-start | bytes 393224 | tf_op jit(solution)/shard_map/rim_coefficients/ppermute | solution.py:398

commit v4 on v3

--- a/solution.py
+++ b/solution.py
@@ -341,11 +341,18 @@
     next_ref, out_ref, high, low, fields, sent,
 ):
     even, fourth, _ = lane_masks(8)
+    rims = [rim_update(rim_ref.at[b], ahead_ref.at[b], arguments_ref[b]) for b in range(8)]
+    for b in range(8):
+        previous = rim_update(before_ref.at[b], behind_ref.at[b], previous_ref[b])
+        levels = zip(rim_bands_back(previous), rim_bands_back(rims[b]))
+        parts = split(jnp.concatenate([rows for first, second in levels for rows in first + second], axis=0))
+        for ref, part in zip((high, low), parts):
+            ref[:, 128 * b + 128 : 128 * b + 256] = part
+            if b == 7:
+                ref[:, 0:128] = part
     copies = []
     for b in range(8):
-        field = fields.at[b]
-        rim = rim_update(rim_ref.at[b], ahead_ref.at[b], arguments_ref[b])
-        previous = rim_update(before_ref.at[b], behind_ref.at[b], previous_ref[b])
+        field, rim = fields.at[b], rims[b]
         field[...] = fresh_ref[b]
         second, third = rim[16:24], rim[24:32]
         field[pl.ds(113, 8, 2), :] = rim[0:8]
@@ -359,12 +366,6 @@
             field[pl.ds(start, 8, 4), :] = jnp.where(mask, value, field[pl.ds(start, 8, 4), :])
         copies.append(pltpu.make_async_copy(field, next_ref.at[0, :, pl.ds(128 * b, 128)], sent.at[b]))
         copies[b].start()
-        levels = zip(rim_bands_back(previous), rim_bands_back(rim))
-        parts = split(jnp.concatenate([rows for first, second in levels for rows in first + second], axis=0))
-        for ref, part in zip((high, low), parts):
-            ref[:, 128 * b + 128 : 128 * b + 256] = part
-            if b == 7:
-                ref[:, 0:128] = part
     add_rows_back(column_product((high, low), RIM_SPANS, back_ref), rows_back_ref, slice(256, 416), out_ref, own_ref)
     for copy in copies:
         copy.wait()

time: 46.2 us -> 46.2 us (level)
  no operation moved by 1% of the time
where the time goes in v4:
time: 46.2 us; the launch traced here: 45.8 us
  blocking collectives  16.5 us (36%)
  starting transfers between devices  11.6 us (25%)
  local copies, waits for them, and re-layouts  6.93 us (15%)
  waiting for transfers between devices  5.03 us (11%)
  Pallas kernels  4.34 us (9%)
  between operations  0.69 us (1%)
  other arithmetic  0.66 us (1%)
    all_to_all x1, blocking collectives, on_device(): adjoint_image = jnp.sum(lax.all_to_all(whole, 'basis', 0, 0), axis=0)  16.5 us
    all_to_all x1, starting transfers between devices, on_device(): lax.all_to_all(jnp.broadcast_to(sky_image, (BASES, ROWS, 128)), 'basis',...  7.59 us
    all_to_all x1, waiting for transfers between devices, on_device(): lax.all_to_all(jnp.broadcast_to(sky_image, (BASES, ROWS, 128)), 'basis',...  4.7 us
    pallas_call x5, Pallas kernels, call(): pl.pallas_call(kernel, in_specs=[vmem] * len(operands), out_specs=out_spe...  4.34 us
    ppermute x3, starting transfers between devices, shifted(): return lax.ppermute(value, 'strip', pairs)  4 us
    squeeze x3, local copies, waits for them, and re-layouts, on_device(): lax.dynamic_index_in_dim(jnp.asarray(m), basis, 0, False)  3.18 us
    unnamed x8, local copies, waits for them, and re-layouts  2.09 us
    broadcast_in_dim x1, local copies, waits for them, and re-layouts, on_device(): jnp.broadcast_to(sky_image, (BASES, ROWS, 128))  1.67 us
  transfers between devices with their start and end apart: 4, of which 2 were waited for; matrix products, arithmetic and copies ran while one was open for 7% of the time, Pallas kernels for 7%

profile of v4, /device:TPU:2, one launch (start us, length us, event | category | flops | bytes accessed | tf_op | source)
XLA Modules:
  0.0 45.8 jit_solution(18128789280677779124)
XLA Ops:
  0.6 1.7 %broadcast_in_dim.3 = f32[8,128,128]{2,1,0:T(8,128)} broadcast(f32[128,128]{1,0:T(8,128)} %param.7), dimensions={1,2} | broadcast | bytes 589824 | tf_op jit(solution)/shard_map/gather_columns/broadcast_in_dim | solution.py:440
  2.3 0.0 copy-start.1
  2.3 0.0 copy-start.3
  2.3 7.6 %all-to-all-start = ((f32[8,128,128]{2,1,0:T(8,128)}), f32[8,128,128]{2,1,0:T(8,128)S(1)}, u32[]{:S(2)}, u32[]{:S(2)}) async-start(f32[8,128,128]{2,1,0:T(8,128)} %broadcast_in_dim.3), calls=%async_computation | async-start | bytes 1048576 | tf_op jit(solution)/shard_map/gather_columns/all_to_all | solution.py:440
  9.9 0.0 copy-start
  9.9 1.0 %copy-done = f32[1,128,1024]{2,1,0:T(8,128)S(1)} copy-done((f32[1,128,1024]{2,1,0:T(8,128)S(1)}, f32[1,128,1024]{2,1,0:T(8,128)}, u32[]{:S(2)}) %copy-start) | copy-done | bytes 524312
  10.9 0.0 copy-start.2
  10.9 1.0 %copy-done.2 = f32[1,128,1024]{2,1,0:T(8,128)S(1)} copy-done((f32[1,128,1024]{2,1,0:T(8,128)S(1)}, f32[1,128,1024]{2,1,0:T(8,128)}, u32[]{:S(2)}) %copy-start.2) | copy-done | bytes 524312
  12.0 0.1 rim_of_arguments.1.arguments_ref
  12.1 0.1 collective-permute-start.2
  12.2 1.0 %dynamic-slice_bitcast_fusion.3.rows_back_ref = bf16[2,128,416]{2,1,0:T(8,128)(2,1)S(1)} fusion(bf16[8,2,128,416]{3,2,1,0:T(8,128)(2,1)} %constant.33.clone, s32[]{:T(128)S(6)} %select_n.9), kind=kLoop, calls=%fused_computation.3 | loop fusion | bytes 425988 | tf_op jit(solution)/shard_map/jit(dynamic_index_in_dim)/squeeze | solution.py:435
  13.2 1.0 %dynamic-slice_bitcast_fusion.2.rows_ref = bf16[2,384,256]{2,1,0:T(8,128)(2,1)S(1)} fusion(bf16[8,2,384,256]{3,2,1,0:T(8,128)(2,1)} %constant.30.clone, s32[]{:T(128)S(6)} %select_n.9), kind=kLoop, calls=%fused_computation.2 | loop fusion | bytes 786436 | tf_op jit(solution)/shard_map/jit(dynamic_index_in_dim)/squeeze | solution.py:435
  14.2 1.2 %dynamic-slice_bitcast_fusion = (bf16[3,256,256]{2,1,0:T(8,128)(2,1)S(1)}, bf16[3,256,256]{2,1,0:T(8,128)(2,1)S(1)}) fusion(bf16[8,3,256,256]{3,2,1,0:T(8,128)(2,1)} %constant.32.clone, s32[]{:T(128)S(6)} %select_n.9, bf16[8,3,256,256]{3,2,1,0:T(8,128)(2,1)} %constant.31.clone), kind=kLoop, calls=%fused_computation | loop fusion | bytes 1572868 | tf_op jit(solution)/shard_map/jit(dynamic_index_in_dim)/squeeze | solution.py:435
  15.4 4.7 %all-to-all-done.image_ref = f32[8,128,128]{2,1,0:T(8,128)S(1)} async-done(((f32[8,128,128]{2,1,0:T(8,128)}), f32[8,128,128]{2,1,0:T(8,128)S(1)}, u32[]{:S(2)}, u32[]{:S(2)}) %all-to-all-start) | async-done | bytes 524320 | tf_op jit(solution)/shard_map/gather_columns/all_to_all | solution.py:440
  20.1 0.8 %rim_coefficients.1 = (f32[8,32,128]{2,1,0:T(8,128)S(1)}, f32[8,32,128]{2,1,0:T(8,128)S(1)}) custom-call(f32[8,128,128]{2,1,0:T(8,128)S(1)} %all-to-all-done.image_ref, bf16[2,384,256]{2,1,0:T(8,128)(2,1)S(1)} %dynamic-slice_bitcast_fusion.2.rows_ref, bf16[3,256,256]{2,1,0:T(8,128)(2,1)S(1)} %get-tuple-element.13.columns_ref), custom_call_target="tpu_custom_call" | custom-call | tf_op jit(solution)/shard_map/rim_coefficients/pallas_call | solution.py:385
  20.9 0.1 collective-permute-start.1
  21.0 3.8 %collective-permute-start = (f32[8,32,128]{2,1,0:T(8,128)S(1)}, f32[8,32,128]{2,1,0:T(8,128)S(1)}, u32[]{:S(2)}, u32[]{:S(2)}) collective-permute-start(f32[8,32,128]{2,1,0:T(8,128)S(1)} %get-tuple-element.17.before_ref), channel_id=1, source_target_pairs={{0,248},{8,0},{16,8},{24,16},{32,24},{40,32},{48,40},{56,48},{64,5... | collective-permute-start | bytes 393224 | tf_op jit(solution)/shard_map/rim_coefficients/ppermute | solution.py:399
  24.8 0.0 copy-done.1
  24.8 0.0 copy-done.3
  24.9 1.0 %own_update.1.fresh_ref = f32[8,128,128]{2,1,0:T(8,128)S(1)} custom-call(f32[8,128,128]{2,1,0:T(8,128)S(1)} %all-to-all-done.image_ref, bf16[2,384,256]{2,1,0:T(8,128)(2,1)S(1)} %dynamic-slice_bitcast_fusion.2.rows_ref, bf16[3,256,256]{2,1,0:T(8,128)(2,1)S(1)} %get-tuple-element.13.columns_ref, f32[1,128,1024]{2,1,0:T(8,128)S(1)} %copy-done.1, ...), custom_call_target="tpu_custom_call" | custom-call | tf_op jit(solution)/shard_map/own_update/pallas_call | solution.py:385
  25.9 1.3 %own_rows.1.own_ref = f32[8,128,128]{2,1,0:T(8,128)S(1)} custom-call(f32[8,128,128]{2,1,0:T(8,128)S(1)} %own_update.1.fresh_ref, bf16[3,256,256]{2,1,0:T(8,128)(2,1)S(1)} %get-tuple-element.14.back_ref, bf16[2,128,416]{2,1,0:T(8,128)(2,1)S(1)} %dynamic-slice_bitcast_fusion.3.rows_back_ref), custom_call_target="tpu_custom_call" | custom-call | tf_op jit(solution)/shard_map/own_rows/pallas_call | solution.py:385
  27.2 0.0 collective-permute-done.2.previous_ref
  27.2 0.3 collective-permute-done.1.behind_ref
  27.5 0.0 collective-permute-done.ahead_ref
  27.5 1.1 %finish.1 = (f32[1,128,1024]{2,1,0:T(8,128)}, f32[8,128,128]{2,1,0:T(8,128)S(1)}) custom-call(f32[8,128,128]{2,1,0:T(8,128)S(1)} %own_rows.1.own_ref, f32[8,128,128]{2,1,0:T(8,128)S(1)} %own_update.1.fresh_ref, f32[8,32,128]{2,1,0:T(8,128)S(1)} %get-tuple-element.16.rim_ref, f32[8,32,128]{2,1,0:T(8,128)S(1)} %collective-permute-done.ahead_ref, ...), custom_call_target="tpu_custom_call" | custom-call | tf_op jit(solution)/shard_map/finish/pallas_call | solution.py:385
  28.6 16.5 %all_to_all.10 = f32[8,128,128]{2,1,0:T(8,128)S(1)} all-to-all(f32[8,128,128]{2,1,0:T(8,128)S(1)} %get-tuple-element.19), channel_id=1, replica_groups=mesh['strip'=32,'basis'=8] {'basis'}, dimensions={0} | all-to-all | bytes 1048576 | tf_op jit(solution)/shard_map/sum_over_bases/all_to_all | solution.py:444
  45.1 0.7 %reduce_sum.9 = f32[128,128]{1,0:T(8,128)} reduce(f32[8,128,128]{2,1,0:T(8,128)S(1)} %all_to_all.10, f32[]{:T(128)} %constant.29.clone.1), dimensions={0}, to_apply=%region_0.1 | reduce | flops 114688 | bytes 589828 | tf_op jit(solution)/shard_map/sum_over_bases/reduce_sum | solution.py:444
Async XLA Ops:
  2.3 22.6 %copy-start.1 = (f32[1,128,1024]{2,1,0:T(8,128)S(1)}, f32[1,128,1024]{2,1,0:T(8,128)}, u32[]{:S(2)}) copy-start(f32[1,128,1024]{2,1,0:T(8,128)} %dual_ref.3) | copy-start | bytes 1572868
  2.3 22.6 %copy-start.3 = (f32[1,128,1024]{2,1,0:T(8,128)S(1)}, f32[1,128,1024]{2,1,0:T(8,128)}, u32[]{:S(2)}) copy-start(f32[1,128,1024]{2,1,0:T(8,128)} %limit_ref.3) | copy-start | bytes 1572868
  2.3 17.8 %all-to-all-start = ((f32[8,128,128]{2,1,0:T(8,128)}), f32[8,128,128]{2,1,0:T(8,128)S(1)}, u32[]{:S(2)}, u32[]{:S(2)}) async-start(f32[8,128,128]{2,1,0:T(8,128)} %broadcast_in_dim.3), calls=%async_computation | async-start | bytes 1048576 | tf_op jit(solution)/shard_map/gather_columns/all_to_all | solution.py:440
  9.9 1.0 %copy-start = (f32[1,128,1024]{2,1,0:T(8,128)S(1)}, f32[1,128,1024]{2,1,0:T(8,128)}, u32[]{:S(2)}) copy-start(f32[1,128,1024]{2,1,0:T(8,128)} %dual_ref.3) | copy-start | bytes 1572868
  10.9 1.0 %copy-start.2 = (f32[1,128,1024]{2,1,0:T(8,128)S(1)}, f32[1,128,1024]{2,1,0:T(8,128)}, u32[]{:S(2)}) copy-start(f32[1,128,1024]{2,1,0:T(8,128)} %limit_ref.3) | copy-start | bytes 1572868
  12.1 15.1 %collective-permute-start.2 = (f32[8,64,128]{2,1,0:T(8,128)S(1)}, f32[8,64,128]{2,1,0:T(8,128)S(1)}, u32[]{:S(2)}, u32[]{:S(2)}) collective-permute-start(f32[8,64,128]{2,1,0:T(8,128)S(1)} %rim_of_arguments.1.arguments_ref), channel_id=1, source_target_pairs={{0,8},{8,16},{16,24},{24,32},{32,40},{40,48},{48,56},{56,64},{64,7... | collective-permute-start | bytes 786440 | tf_op jit(solution)/shard_map/rim_of_arguments/ppermute | solution.py:399
  20.9 6.6 %collective-permute-start.1 = (f32[8,32,128]{2,1,0:T(8,128)S(1)}, f32[8,32,128]{2,1,0:T(8,128)S(1)}, u32[]{:S(2)}, u32[]{:S(2)}) collective-permute-start(f32[8,32,128]{2,1,0:T(8,128)S(1)} %get-tuple-element.16.rim_ref), channel_id=1, source_target_pairs={{0,8},{8,16},{16,24},{24,32},{32,40},{40,48},{48,56},{56,64},{64,7... | collective-permute-start | bytes 393224 | tf_op jit(solution)/shard_map/rim_coefficients/ppermute | solution.py:399
  21.0 6.5 %collective-permute-start = (f32[8,32,128]{2,1,0:T(8,128)S(1)}, f32[8,32,128]{2,1,0:T(8,128)S(1)}, u32[]{:S(2)}, u32[]{:S(2)}) collective-permute-start(f32[8,32,128]{2,1,0:T(8,128)S(1)} %get-tuple-element.17.before_ref), channel_id=1, source_target_pairs={{0,248},{8,0},{16,8},{24,16},{32,24},{40,32},{48,40},{56,48},{64,5... | collective-permute-start | bytes 393224 | tf_op jit(solution)/shard_map/rim_coefficients/ppermute | solution.py:399
